TPU v7x, 512 devices: a whole 4x8x8 slice. The times are simulated.
512 devices in a mesh: grp: 32 (over z, x_lo, core), dp: 16 (over x_hi, y).
Axes of the slice: x: 4 (x_hi: 2, x_lo: 2; x = x_hi * 2 + x_lo), y: 8, z: 8, core: 2. Of those that a mesh axis runs over, the one named last changes fastest.
Arguments:
- q_rows: bfloat16 [65536, 4096], P(('grp', 'dp')), may hold values from -6 to 6
- k_rows: bfloat16 [65536, 1024], P(('grp', 'dp')), may hold values from -6 to 6
- value_rows: bfloat16 [65536, 1024], P(('grp', 'dp')), may hold values from -6 to 6
- grad_out: bfloat16 [65536, 4096], P(('grp', 'dp')), may hold values from -6 to 6
- lengths: int32 [16, 4, 4], P('dp'), may hold values from 0 to 1024, as said below
- send_rows: int32 [512, 16, 12], P(('grp', 'dp')), may hold values from -1 to 127, as said below
- recv_slots: int32 [16, 4096], P('dp', 'grp'), may hold values from 0 to 191, as said below
Outputs:
- grad_q: bfloat16 [65536, 4096], P(('grp', 'dp'))
- key_gradient: bfloat16 [65536, 1024], P(('grp', 'dp'))
- value_gradient: bfloat16 [65536, 1024], P(('grp', 'dp'))
Inputs may be any that keep to these rules, and one draw needn't show every extreme that they name: Entry [e, t] holds the lengths of the sequences packed in order into column (e, t); they sum to 1024, trailing entries are 0, and some column holds a single sequence of 1024. `send_rows`: row g * 16 + d lists for every dp index the local rows that the device of grp index g and dp index d sends there, -1 marking an empty slot; each local row is listed exactly once, and every device fills all 12 slots for some dp index. `recv_slots`: entry [e, P] names the slot d * 12 + c (sender d along dp, its slot c) whose row takes position P on the device of grp index P // 128 and dp index e; every filled slot is named exactly once and no empty one.
All inputs are finite; a program needn't handle non-finite values.
Results may differ from a plain program's by a relative error of at most 0.014.
Values may be sent and summed in bfloat16 or wider, within the bound.
No kernel may reach another device: no remote copies, remote signals or barrier semaphores. Data moves between devices by JAX's collectives and lax.ppermute only.
A program may use at most 128 MiB of HBM per device.

v0:
```python
import math

import jax
import jax.numpy as jnp
from jax import lax
from jax.sharding import PartitionSpec as P

QUERY_HEADS = 32
KEY_VALUE_HEADS = 8
HEAD_DIM = 128
SHARERS_PER_COL = 8


def from_partner(value, axis, apart):
    mask = 2**apart
    pairs = [(source, source ^ mask) for source in range(lax.axis_size(axis))]
    return lax.ppermute(value, axis, pairs)


def pair_sections(bundle, member, send_half):
    sections = bundle.shape[0].bit_length() - 1
    cube = bundle.reshape((2,) * sections + bundle.shape[1:])
    for bit in range(sections):
        axis_pos = sections - 1 - bit
        other = 1 - (member >> bit & 1)
        half = lax.dynamic_index_in_dim(cube, other, axis_pos, keepdims=True)
        cube = lax.dynamic_update_index_in_dim(cube, send_half(half, bit), other, axis_pos)
    return cube.reshape(bundle.shape)


def body(q_rows, k_rows, value_rows, grad_out, lengths, send_rows, recv_slots):
    count_of_rows = q_rows.shape[0]
    n_dp = lax.axis_size("dp")
    plan_out = send_rows[0]
    slot_count = plan_out.shape[1]
    slot_list = recv_slots[0]
    picked = jnp.clip(plan_out, 0, count_of_rows - 1).reshape(-1)
    q_heads = QUERY_HEADS // SHARERS_PER_COL
    shared_heads = KEY_VALUE_HEADS // SHARERS_PER_COL
    per_shared_head = q_heads // shared_heads
    query_width = q_heads * HEAD_DIM
    key_value_width = shared_heads * HEAD_DIM
    column = SHARERS_PER_COL * count_of_rows
    block_len = min(512, column)
    block_count = column // block_len
    turns = block_count * q_heads
    score_scale = 1.0 / math.sqrt(HEAD_DIM)
    grp_place = lax.axis_index("grp")
    member = grp_place % SHARERS_PER_COL
    group_index = grp_place // SHARERS_PER_COL

    def outgoing(source):
        return jnp.take(source, picked, axis=0).reshape(n_dp, slot_count, source.shape[1])

    def incoming(arrived):
        return jnp.take(arrived.reshape(n_dp * slot_count, arrived.shape[2]), slot_list, axis=0)

    def by_member(source, width):
        return jnp.transpose(source.reshape(count_of_rows, SHARERS_PER_COL, width), (1, 0, 2))

    query_column, key_column, value_column, output_grad_column = (
        lax.all_to_all(outgoing(q_rows), "dp", split_axis=0, concat_axis=0, tiled=True),
        lax.all_to_all(outgoing(k_rows), "dp", split_axis=0, concat_axis=0, tiled=True),
        lax.all_to_all(outgoing(value_rows), "dp", split_axis=0, concat_axis=0, tiled=True),
        lax.all_to_all(outgoing(grad_out), "dp", split_axis=0, concat_axis=0, tiled=True),
    )

    def pass_all(half, bit):
        return from_partner(half, "grp", bit)

    pairs = (
        (query_column, query_width),
        (key_column, key_value_width),
        (value_column, key_value_width),
        (output_grad_column, query_width),
    )
    arrived = pair_sections(
        jnp.concatenate([by_member(incoming(arrived), width) for arrived, width in pairs], axis=2),
        member,
        pass_all,
    )
    widths = (query_width, key_value_width, key_value_width, query_width)
    flat = arrived.reshape(column, arrived.shape[2])
    pieces = []
    offset = 0
    for width in widths:
        pieces.append(flat[:, offset : offset + width])
        offset = offset + width
    q_head, k_head, v_head, g_head = pieces
    own_lengths = lengths[0][group_index]
    seq_ends = jnp.cumsum(own_lengths, dtype=jnp.int32)
    position = jnp.arange(column, dtype=jnp.int32)
    segment = jnp.sum(
        (seq_ends[None, :] <= position[:, None]).astype(jnp.int32), axis=1, dtype=jnp.int32
    )
    query_pos = position.reshape(block_count, block_len)
    allowed = (segment.reshape(block_count, block_len)[:, :, None] == segment[None, None, :]) & (
        position[None, None, :] <= query_pos[:, :, None]
    )
    q_view = q_head.reshape(block_count, block_len, q_heads, HEAD_DIM)
    key_view = k_head.reshape(column, shared_heads, HEAD_DIM)
    value_view = v_head.reshape(column, shared_heads, HEAD_DIM)
    indices = jnp.arange(turns, dtype=jnp.int32)

    def turn_inputs(index):
        block = index // q_heads
        head = index % q_heads
        kv_index = head // per_shared_head
        return (
            block,
            head,
            q_view[block, :, head],
            key_view[:, kv_index],
            value_view[:, kv_index],
            allowed[block],
        )

    def scores_of(query_part, key_part, mask_part):
        raw = (
            jnp.einsum("md,kd->mk", query_part, key_part, preferred_element_type=jnp.float32)
            * score_scale
        )
        return jnp.where(mask_part, raw, -jnp.inf)

    def forward_turn(index):
        block, head, query_part, key_part, value_part, mask_part = turn_inputs(index)
        scores = scores_of(query_part, key_part, mask_part)
        row_max = jnp.max(scores, axis=-1, keepdims=True)
        shifted = jnp.exp(scores - row_max)
        row_sum = jnp.sum(shifted, axis=-1, keepdims=True)
        weights_b = (shifted / row_sum).astype(jnp.bfloat16)
        attended = jnp.einsum(
            "mk,kd->md", weights_b, value_part, preferred_element_type=jnp.float32
        ).astype(jnp.bfloat16)
        return (attended, weights_b)

    saved = lax.map(forward_turn, indices)
    g_view = g_head.reshape(block_count, block_len, q_heads, HEAD_DIM)

    def backward_turn(parts):
        index, attended_part, kept = parts
        block, head, query_part, key_part, value_part, mask_part = turn_inputs(index)
        grad_part = g_view[block, :, head]
        row_delta = jnp.sum(
            grad_part.astype(jnp.float32) * attended_part.astype(jnp.float32), axis=-1
        )
        weights_b = kept[0]
        d_weights = jnp.einsum(
            "md,kd->mk", grad_part, value_part, preferred_element_type=jnp.float32
        )
        dscore = (weights_b.astype(jnp.float32) * (d_weights - row_delta[:, None])).astype(
            jnp.bfloat16
        )
        query_gradient = (
            jnp.einsum("mk,kd->md", dscore, key_part, preferred_element_type=jnp.float32)
            * score_scale
        ).astype(jnp.bfloat16)
        key_window = (
            jnp.einsum("mk,md->kd", dscore, query_part, preferred_element_type=jnp.float32)
            * score_scale
        )
        value_window = jnp.einsum(
            "mk,md->kd", weights_b, grad_part, preferred_element_type=jnp.float32
        )
        return (query_gradient, key_window, value_window)

    results = lax.map(backward_turn, (indices, saved[0], saved[1:]))
    query_gradient = jnp.transpose(
        results[0].reshape(block_count, q_heads, block_len, HEAD_DIM), (0, 2, 1, 3)
    ).reshape(column, query_width)

    def folded(windows):
        per_head = jnp.sum(windows.reshape(block_count, q_heads, column, HEAD_DIM), axis=0)
        heads = (
            jnp.transpose(per_head, (1, 0, 2))
            .astype(jnp.bfloat16)
            .reshape(column, shared_heads, per_shared_head, HEAD_DIM)
        )
        return (
            jnp.sum(heads.astype(jnp.float32), axis=2)
            .astype(jnp.bfloat16)
            .reshape(column, key_value_width)
        )

    back_width = query_width + 2 * key_value_width
    back_bundle = jnp.concatenate(
        [query_gradient, folded(results[1]), folded(results[2])], axis=1
    ).reshape(SHARERS_PER_COL, count_of_rows, back_width)

    def pass_back(half, bit):
        return from_partner(half, "grp", bit)

    returned_rows = jnp.transpose(pair_sections(back_bundle, member, pass_back), (1, 0, 2))
    dq_col = returned_rows[:, :, :query_width].reshape(count_of_rows, QUERY_HEADS * HEAD_DIM)
    key_grad_column = returned_rows[:, :, query_width : query_width + key_value_width].reshape(
        count_of_rows, KEY_VALUE_HEADS * HEAD_DIM
    )
    value_grad_column = returned_rows[:, :, query_width + key_value_width :].reshape(
        count_of_rows, KEY_VALUE_HEADS * HEAD_DIM
    )

    def back_buffer(source):
        return (
            jnp.zeros((n_dp * slot_count, source.shape[1]), source.dtype)
            .at[slot_list]
            .set(source)
            .reshape(n_dp, slot_count, source.shape[1])
        )

    home_q, home_k, home_v = (
        lax.all_to_all(back_buffer(dq_col), "dp", split_axis=0, concat_axis=0, tiled=True),
        lax.all_to_all(back_buffer(key_grad_column), "dp", split_axis=0, concat_axis=0, tiled=True),
        lax.all_to_all(
            back_buffer(value_grad_column), "dp", split_axis=0, concat_axis=0, tiled=True
        ),
    )
    row_places = jnp.where(plan_out >= 0, plan_out, count_of_rows).reshape(-1)

    def settle(arrived):
        return (
            jnp.zeros((count_of_rows, arrived.shape[2]), arrived.dtype)
            .at[row_places]
            .set(arrived.reshape(n_dp * slot_count, arrived.shape[2]), mode="drop")
        )

    return (settle(home_q), settle(home_k), settle(home_v))


def solution(mesh):
    placed = (
        P(("grp", "dp"), None),
        P(("grp", "dp"), None),
        P(("grp", "dp"), None),
        P(("grp", "dp"), None),
        P("dp", None, None),
        P(("grp", "dp"), None, None),
        P("dp", "grp"),
    )
    return jax.shard_map(
        body,
        mesh=mesh,
        in_specs=placed,
        out_specs=(P(("grp", "dp"), None), P(("grp", "dp"), None), P(("grp", "dp"), None)),
        check_vma=False,
    )
```

profile of v0, /device:TPU:1, one launch (start us, length us, event | category | flops | bytes accessed | tf_op | source)
XLA Modules:
  0.0 561.0 jit_solution(10199504447461530686)
XLA Ops:
  6.0 10.2 %all-to-all-start.1 = ((bf16[16,12,1024]{2,1,0:T(8,128)(2,1)}), bf16[16,12,1024]{2,1,0:T(8,128)(2,1)S(1)}, u32[]{:S(2)}, u32[]{:S(2)}) async-start(bf16[16,12,1024]{2,1,0:T(8,128)(2,1)} %reshape.243), calls=%async_computation.1 | async-start | bytes 1048576 | tf_op jit(solution)/shard_map/all_to_all | solution.py:63
  22.5 9.0 %all-to-all-done.1 = bf16[16,12,1024]{2,1,0:T(8,128)(2,1)S(1)} async-done(((bf16[16,12,1024]{2,1,0:T(8,128)(2,1)}), bf16[16,12,1024]{2,1,0:T(8,128)(2,1)S(1)}, u32[]{:S(2)}, u32[]{:S(2)}) %all-to-all-start.1) | async-done | bytes 393248 | tf_op jit(solution)/shard_map/all_to_all | solution.py:63
  32.3 6.0 %all-to-all-start.2 = ((bf16[16,12,1024]{2,1,0:T(8,128)(2,1)}), bf16[16,12,1024]{2,1,0:T(8,128)(2,1)}, u32[]{:S(2)}, u32[]{:S(2)}) async-start(bf16[16,12,1024]{2,1,0:T(8,128)(2,1)} %reshape.246), calls=%async_computation.2 | async-start | bytes 1048576 | tf_op jit(solution)/shard_map/all_to_all | solution.py:64
  42.7 9.8 %all-to-all-done.2 = bf16[16,12,1024]{2,1,0:T(8,128)(2,1)} async-done(((bf16[16,12,1024]{2,1,0:T(8,128)(2,1)}), bf16[16,12,1024]{2,1,0:T(8,128)(2,1)}, u32[]{:S(2)}, u32[]{:S(2)}) %all-to-all-start.2) | async-done | bytes 393248 | tf_op jit(solution)/shard_map/all_to_all | solution.py:64
  52.5 6.3 %all-to-all-start.3 = ((bf16[16,12,4096]{2,1,0:T(8,128)(2,1)}), bf16[16,12,4096]{2,1,0:T(8,128)(2,1)S(1)}, u32[]{:S(2)}, u32[]{:S(2)}) async-start(bf16[16,12,4096]{2,1,0:T(8,128)(2,1)} %reshape.249), calls=%async_computation.3 | async-start | bytes 4194304 | tf_op jit(solution)/shard_map/all_to_all | solution.py:65
  62.3 45.1 %all-to-all-done.3 = bf16[16,12,4096]{2,1,0:T(8,128)(2,1)S(1)} async-done(((bf16[16,12,4096]{2,1,0:T(8,128)(2,1)}), bf16[16,12,4096]{2,1,0:T(8,128)(2,1)S(1)}, u32[]{:S(2)}, u32[]{:S(2)}) %all-to-all-start.3) | async-done | bytes 1572896 | tf_op jit(solution)/shard_map/all_to_all | solution.py:65
  107.4 6.3 %all-to-all-start = ((bf16[16,12,4096]{2,1,0:T(8,128)(2,1)}), bf16[16,12,4096]{2,1,0:T(8,128)(2,1)}, u32[]{:S(2)}, u32[]{:S(2)}) async-start(bf16[16,12,4096]{2,1,0:T(8,128)(2,1)} %reshape.240), calls=%async_computation | async-start | bytes 4194304 | tf_op jit(solution)/shard_map/all_to_all | solution.py:62
  120.6 41.4 %all-to-all-done = bf16[16,12,4096]{2,1,0:T(8,128)(2,1)} async-done(((bf16[16,12,4096]{2,1,0:T(8,128)(2,1)}), bf16[16,12,4096]{2,1,0:T(8,128)(2,1)}, u32[]{:S(2)}, u32[]{:S(2)}) %all-to-all-start) | async-done | bytes 1572896 | tf_op jit(solution)/shard_map/all_to_all | solution.py:62
  170.9 5.8 %collective-permute-start = (bf16[2,2,1,128,1280]{4,3,2,1,0:T(8,128)(2,1)}, bf16[2,2,1,128,1280]{4,3,2,1,0:T(8,128)(2,1)}, u32[]{:S(2)}, u32[]{:S(2)}) collective-permute-start(bf16[2,2,1,128,1280]{4,3,2,1,0:T(8,128)(2,1)} %constant_dynamic-slice_fusion.5), channel_id=1, source_target_pairs={{0,16},{16,0},{32,48},{48,32},{64,80},{80,64},{96,112},{112,96},{1... | collective-permute-start | bytes 3932168 | tf_op jit(solution)/shard_map/ppermute | solution.py:17
  184.4 30.0 %collective-permute-done.1 = bf16[2,1,2,128,1280]{4,3,2,1,0:T(8,128)(2,1)} collective-permute-done((bf16[2,1,2,128,1280]{4,3,2,1,0:T(8,128)(2,1)}, bf16[2,1,2,128,1280]{4,3,2,1,0:T(8,128)(2,1)}, u32[]{:S(2)}, u32[]{:S(2)}) %collective-permute-start.1) | collective-permute-done | bytes 1310752 | tf_op jit(solution)/shard_map/ppermute | solution.py:17
  217.0 4.2 collective-permute-start.2
  224.2 25.0 %collective-permute-done.2 = bf16[1,2,2,128,1280]{4,3,2,1,0:T(8,128)(2,1)} collective-permute-done((bf16[1,2,2,128,1280]{4,3,2,1,0:T(8,128)(2,1)}, bf16[1,2,2,128,1280]{4,3,2,1,0:T(8,128)(2,1)}, u32[]{:S(2)}, u32[]{:S(2)}) %collective-permute-start.2) | collective-permute-done | bytes 1310752 | tf_op jit(solution)/shard_map/ppermute | solution.py:17
  257.0 55.2 %while.30 = (s32[]{:T(128)}, bf16[8,512,128]{2,1,0:T(8,128)(2,1)}, bf16[8,512,1024]{2,1,0:T(8,128)(2,1)}, s32[8]{0:T(128)S(1)}, pred[2,512,1024]{2,1,0:T(32,128)...) while((s32[]{:T(128)}, bf16[8,512,128]{2,1,0:T(8,128)(2,1)}, ...), condition=%wide.region_5.10_spmd, body=%wide.region_2.9_spmd.sunk | while | flops 274267168 | bytes 10765200 | solution.py:137
  316.8 86.5 %while.31 = (s32[]{:T(128)}, bf16[8,512,128]{2,1,0:T(8,128)(2,1)}, f32[8,1024,128]{2,1,0:T(8,128)}, f32[8,1024,128]{2,1,0:T(8,128)}, bf16[8,512,1024]{2,1,0:T(8,...) while((s32[]{:T(128)}, bf16[8,512,128]{2,1,0:T(8,128)(2,1)}, ...), condition=%wide.region_8.13_spmd, body=%wide.region_6.12_spmd.sunk | while | flops 539491840 | bytes 7608784 | solution.py:167
  411.8 3.7 collective-permute-start.3
  419.8 18.4 %collective-permute-done.4 = bf16[2,1,2,128,768]{4,3,2,1,0:T(8,128)(2,1)S(1)} collective-permute-done((bf16[2,1,2,128,768]{4,3,2,1,0:T(8,128)(2,1)S(1)}, bf16[2,1,2,128,768]{4,3,2,1,0:T(8,128)(2,1)S(1)}, u32[]{:S(2)}, u32[]{:S(2)}) %collective-permute-start.4) | collective-permute-done | bytes 786464 | tf_op jit(solution)/shard_map/ppermute | solution.py:17
  441.8 16.4 %collective-permute-done.5 = bf16[1,2,2,128,768]{4,3,2,1,0:T(8,128)(2,1)S(1)} collective-permute-done((bf16[1,2,2,128,768]{4,3,2,1,0:T(8,128)(2,1)S(1)}, bf16[1,2,2,128,768]{4,3,2,1,0:T(8,128)(2,1)S(1)}, u32[]{:S(2)}, u32[]{:S(2)}) %collective-permute-start.5) | collective-permute-done | bytes 786464 | tf_op jit(solution)/shard_map/ppermute | solution.py:17
  460.5 4.5 all-to-all-start.5
  467.1 11.7 %all-to-all-done.5 = bf16[16,12,1024]{2,1,0:T(8,128)(2,1)S(1)} async-done(((bf16[16,12,1024]{2,1,0:T(8,128)(2,1)}), bf16[16,12,1024]{2,1,0:T(8,128)(2,1)S(1)}, u32[]{:S(2)}, u32[]{:S(2)}) %all-to-all-start.5) | async-done | bytes 393248 | tf_op jit(solution)/shard_map/all_to_all | solution.py:212
  478.8 6.7 %all-to-all-start.6 = ((bf16[16,12,1024]{2,1,0:T(8,128)(2,1)}), bf16[16,12,1024]{2,1,0:T(8,128)(2,1)S(1)}, u32[]{:S(2)}, u32[]{:S(2)}) async-start(bf16[16,12,1024]{2,1,0:T(8,128)(2,1)} %reshape.268), calls=%async_computation.6 | async-start | bytes 1048576 | tf_op jit(solution)/shard_map/all_to_all | solution.py:213
  491.5 8.3 %all-to-all-done.6 = bf16[16,12,1024]{2,1,0:T(8,128)(2,1)S(1)} async-done(((bf16[16,12,1024]{2,1,0:T(8,128)(2,1)}), bf16[16,12,1024]{2,1,0:T(8,128)(2,1)S(1)}, u32[]{:S(2)}, u32[]{:S(2)}) %all-to-all-start.6) | async-done | bytes 393248 | tf_op jit(solution)/shard_map/all_to_all | solution.py:213
  500.5 6.3 %all-to-all-start.4 = ((bf16[16,12,4096]{2,1,0:T(8,128)(2,1)}), bf16[16,12,4096]{2,1,0:T(8,128)(2,1)S(1)}, u32[]{:S(2)}, u32[]{:S(2)}) async-start(bf16[16,12,4096]{2,1,0:T(8,128)(2,1)} %reshape.262), calls=%async_computation.4 | async-start | bytes 4194304 | tf_op jit(solution)/shard_map/all_to_all | solution.py:211
  512.4 42.7 %all-to-all-done.4 = bf16[16,12,4096]{2,1,0:T(8,128)(2,1)S(1)} async-done(((bf16[16,12,4096]{2,1,0:T(8,128)(2,1)}), bf16[16,12,4096]{2,1,0:T(8,128)(2,1)S(1)}, u32[]{:S(2)}, u32[]{:S(2)}) %all-to-all-start.4) | async-done | bytes 1572896 | tf_op jit(solution)/shard_map/all_to_all | solution.py:211
  556.5 4.6 scatter_custom_fusion.1
  (212 shorter events, 195.4 us)
Async XLA Ops:
  0.6 15.6 %copy-start = (bf16[128,4096]{1,0:T(8,128)(2,1)S(1)}, bf16[128,4096]{1,0:T(8,128)(2,1)}, u32[]{:S(2)}) copy-start(bf16[128,4096]{1,0:T(8,128)(2,1)} %param.22) | copy-start | bytes 3145732
  0.6 3.3 copy-start.3
  6.0 25.5 %all-to-all-start.1 = ((bf16[16,12,1024]{2,1,0:T(8,128)(2,1)}), bf16[16,12,1024]{2,1,0:T(8,128)(2,1)S(1)}, u32[]{:S(2)}, u32[]{:S(2)}) async-start(bf16[16,12,1024]{2,1,0:T(8,128)(2,1)} %reshape.243), calls=%async_computation.1 | async-start | bytes 1048576 | tf_op jit(solution)/shard_map/all_to_all | solution.py:63
  16.3 2.7 copy-start.2
  21.7 16.6 %copy-start.6 = (bf16[192,4096]{1,0:T(8,128)(2,1)S(1)}, bf16[192,4096]{1,0:T(8,128)(2,1)}, u32[]{:S(2)}) copy-start(bf16[192,4096]{1,0:T(8,128)(2,1)} %gather_fusion.6) | copy-start | bytes 4718596
  32.3 20.2 %all-to-all-start.2 = ((bf16[16,12,1024]{2,1,0:T(8,128)(2,1)}), bf16[16,12,1024]{2,1,0:T(8,128)(2,1)}, u32[]{:S(2)}, u32[]{:S(2)}) async-start(bf16[16,12,1024]{2,1,0:T(8,128)(2,1)} %reshape.246), calls=%async_computation.2 | async-start | bytes 1048576 | tf_op jit(solution)/shard_map/all_to_all | solution.py:64
  52.5 54.8 %all-to-all-start.3 = ((bf16[16,12,4096]{2,1,0:T(8,128)(2,1)}), bf16[16,12,4096]{2,1,0:T(8,128)(2,1)S(1)}, u32[]{:S(2)}, u32[]{:S(2)}) async-start(bf16[16,12,4096]{2,1,0:T(8,128)(2,1)} %reshape.249), calls=%async_computation.3 | async-start | bytes 4194304 | tf_op jit(solution)/shard_map/all_to_all | solution.py:65
  62.3 51.4 %copy-start.13 = (s32[1,128]{1,0:T(1,128)S(1)}, s32[1,128]{1,0:T(1,128)}, u32[]{:S(2)}) copy-start(s32[1,128]{1,0:T(1,128)} %param.25) | copy-start | bytes 1540
  62.3 51.5 %copy-start.8 = (bf16[16,12,1024]{2,1,0:T(8,128)(2,1)S(1)}, bf16[16,12,1024]{2,1,0:T(8,128)(2,1)}, u32[]{:S(2)}) copy-start(bf16[16,12,1024]{2,1,0:T(8,128)(2,1)} %copy-done.7) | copy-start | bytes 1179652
  107.4 6.4 %copy-start.5 = (bf16[16,12,4096]{2,1,0:T(8,128)(2,1)}, bf16[16,12,4096]{2,1,0:T(8,128)(2,1)S(1)}, u32[]{:S(2)}) copy-start(bf16[16,12,4096]{2,1,0:T(8,128)(2,1)S(1)} %all-to-all-done.3) | copy-start | bytes 4718596
  107.4 54.7 %all-to-all-start = ((bf16[16,12,4096]{2,1,0:T(8,128)(2,1)}), bf16[16,12,4096]{2,1,0:T(8,128)(2,1)}, u32[]{:S(2)}, u32[]{:S(2)}) async-start(bf16[16,12,4096]{2,1,0:T(8,128)(2,1)} %reshape.240), calls=%async_computation | async-start | bytes 4194304 | tf_op jit(solution)/shard_map/all_to_all | solution.py:62
  170.9 8.7 %collective-permute-start = (bf16[2,2,1,128,1280]{4,3,2,1,0:T(8,128)(2,1)}, bf16[2,2,1,128,1280]{4,3,2,1,0:T(8,128)(2,1)}, u32[]{:S(2)}, u32[]{:S(2)}) collective-permute-start(bf16[2,2,1,128,1280]{4,3,2,1,0:T(8,128)(2,1)} %constant_dynamic-slice_fusion.5), channel_id=1, source_target_pairs={{0,16},{16,0},{32,48},{48,32},{64,80},{80,64},{96,112},{112,96},{1... | collective-permute-start | bytes 3932168 | tf_op jit(solution)/shard_map/ppermute | solution.py:17
  182.2 32.2 %collective-permute-start.1 = (bf16[2,1,2,128,1280]{4,3,2,1,0:T(8,128)(2,1)}, bf16[2,1,2,128,1280]{4,3,2,1,0:T(8,128)(2,1)}, u32[]{:S(2)}, u32[]{:S(2)}) collective-permute-start(bf16[2,1,2,128,1280]{4,3,2,1,0:T(8,128)(2,1)} %constant_dynamic-slice_fusion.4), channel_id=1, source_target_pairs={{0,32},{16,48},{32,0},{48,16},{64,96},{80,112},{96,64},{112,80},{1... | collective-permute-start | bytes 3932168 | tf_op jit(solution)/shard_map/ppermute | solution.py:17
  217.0 32.2 %collective-permute-start.2 = (bf16[1,2,2,128,1280]{4,3,2,1,0:T(8,128)(2,1)}, bf16[1,2,2,128,1280]{4,3,2,1,0:T(8,128)(2,1)}, u32[]{:S(2)}, u32[]{:S(2)}) collective-permute-start(bf16[1,2,2,128,1280]{4,3,2,1,0:T(8,128)(2,1)} %constant_dynamic-slice_fusion.3), channel_id=1, source_target_pairs={{0,64},{16,80},{32,96},{48,112},{64,0},{80,16},{96,32},{112,48},{1... | collective-permute-start | bytes 3932168 | tf_op jit(solution)/shard_map/ppermute | solution.py:17
  411.8 5.6 %collective-permute-start.3 = (bf16[2,2,1,128,768]{4,3,2,1,0:T(8,128)(2,1)S(1)}, bf16[2,2,1,128,768]{4,3,2,1,0:T(8,128)(2,1)S(1)}, u32[]{:S(2)}, u32[]{:S(2)}) collective-permute-start(bf16[2,2,1,128,768]{4,3,2,1,0:T(8,128)(2,1)S(1)} %constant_dynamic-slice_fusion.2), channel_id=1, source_target_pairs={{0,16},{16,0},{32,48},{48,32},{64,80},{80,64},{96,112},{112,96},{1... | collective-permute-start | bytes 2359304 | tf_op jit(solution)/shard_map/ppermute | solution.py:17
  417.6 20.6 %collective-permute-start.4 = (bf16[2,1,2,128,768]{4,3,2,1,0:T(8,128)(2,1)S(1)}, bf16[2,1,2,128,768]{4,3,2,1,0:T(8,128)(2,1)S(1)}, u32[]{:S(2)}, u32[]{:S(2)}) collective-permute-start(bf16[2,1,2,128,768]{4,3,2,1,0:T(8,128)(2,1)S(1)} %constant_dynamic-slice_fusion.1), channel_id=1, source_target_pairs={{0,32},{16,48},{32,0},{48,16},{64,96},{80,112},{96,64},{112,80},{1... | collective-permute-start | bytes 2359304 | tf_op jit(solution)/shard_map/ppermute | solution.py:17
  438.4 19.7 %collective-permute-start.5 = (bf16[1,2,2,128,768]{4,3,2,1,0:T(8,128)(2,1)S(1)}, bf16[1,2,2,128,768]{4,3,2,1,0:T(8,128)(2,1)S(1)}, u32[]{:S(2)}, u32[]{:S(2)}) collective-permute-start(bf16[1,2,2,128,768]{4,3,2,1,0:T(8,128)(2,1)S(1)} %constant_dynamic-slice_fusion), channel_id=1, source_target_pairs={{0,64},{16,80},{32,96},{48,112},{64,0},{80,16},{96,32},{112,48},{1... | collective-permute-start | bytes 2359304 | tf_op jit(solution)/shard_map/ppermute | solution.py:17
  460.5 18.4 %all-to-all-start.5 = ((bf16[16,12,1024]{2,1,0:T(8,128)(2,1)}), bf16[16,12,1024]{2,1,0:T(8,128)(2,1)S(1)}, u32[]{:S(2)}, u32[]{:S(2)}) async-start(bf16[16,12,1024]{2,1,0:T(8,128)(2,1)} %reshape.265), calls=%async_computation.5 | async-start | bytes 1048576 | tf_op jit(solution)/shard_map/all_to_all | solution.py:212
  478.8 7.9 %copy-start.9 = (bf16[16,12,1024]{2,1,0:T(8,128)(2,1)}, bf16[16,12,1024]{2,1,0:T(8,128)(2,1)S(1)}, u32[]{:S(2)}) copy-start(bf16[16,12,1024]{2,1,0:T(8,128)(2,1)S(1)} %all-to-all-done.5) | copy-start | bytes 1179652
  478.8 20.9 %all-to-all-start.6 = ((bf16[16,12,1024]{2,1,0:T(8,128)(2,1)}), bf16[16,12,1024]{2,1,0:T(8,128)(2,1)S(1)}, u32[]{:S(2)}, u32[]{:S(2)}) async-start(bf16[16,12,1024]{2,1,0:T(8,128)(2,1)} %reshape.268), calls=%async_computation.6 | async-start | bytes 1048576 | tf_op jit(solution)/shard_map/all_to_all | solution.py:213
  491.5 15.4 %copy-start.12 = (s32[1,16,12]{1,0,2:T(1,128)S(1)}, s32[1,16,12]{1,0,2:T(1,128)}, u32[]{:S(2)}) copy-start(s32[1,16,12]{1,0,2:T(1,128)} %param.24) | copy-start | bytes 2308
  491.5 15.6 %copy-start.10 = (bf16[16,12,1024]{2,1,0:T(8,128)(2,1)S(1)}, bf16[16,12,1024]{2,1,0:T(8,128)(2,1)}, u32[]{:S(2)}) copy-start(bf16[16,12,1024]{2,1,0:T(8,128)(2,1)} %copy-done.9) | copy-start | bytes 1179652
  500.5 54.6 %all-to-all-start.4 = ((bf16[16,12,4096]{2,1,0:T(8,128)(2,1)}), bf16[16,12,4096]{2,1,0:T(8,128)(2,1)S(1)}, u32[]{:S(2)}, u32[]{:S(2)}) async-start(bf16[16,12,4096]{2,1,0:T(8,128)(2,1)} %reshape.262), calls=%async_computation.4 | async-start | bytes 4194304 | tf_op jit(solution)/shard_map/all_to_all | solution.py:211
  510.4 50.7 %copy-start.1 = (bf16[128,4096]{1,0:T(8,128)(2,1)S(1)}, bf16[128,4096]{1,0:T(8,128)(2,1)}, u32[]{:S(2)}) copy-start(bf16[128,4096]{1,0:T(8,128)(2,1)} %param.22) | copy-start | bytes 3145732
  (3 other events, 4.2 us)
where the time goes:
time: 566 us; the launch traced here: 561 us
  waiting for transfers between devices  263 us (46%)
  local copies, waits for them, and re-layouts  83 us (15%)
  starting transfers between devices  67.8 us (12%)
  matrix products  66.4 us (12%)
  loops' own time  42 us (7%)
  other arithmetic  37.9 us (7%)
    ppermute x6, waiting for transfers between devices, from_partner(): return lax.ppermute(value, axis, pairs)  94.6 us
    all_to_all x1, waiting for transfers between devices, body(): lax.all_to_all(outgoing(grad_out), 'dp', split_axis=0, concat_axis=0, til...  45.1 us
    all_to_all x1, waiting for transfers between devices, body(): lax.all_to_all(back_buffer(dq_col), 'dp', split_axis=0, concat_axis=0, ti...  42.7 us
    all_to_all x1, waiting for transfers between devices, body(): lax.all_to_all(outgoing(q_rows), 'dp', split_axis=0, concat_axis=0, tiled...  41.4 us
    ppermute x6, starting transfers between devices, from_partner(): return lax.ppermute(value, axis, pairs)  21.4 us
    another operation x1, loops' own time, body(): results = lax.map(backward_turn, (indices, saved[0], saved[1:]))  21.1 us
    another operation x1, loops' own time, body(): saved = lax.map(forward_turn, indices)  21 us
    dot_general x8, matrix products, backward_turn(): jnp.einsum('mk,md->kd', weights_b, grad_part, preferred_element_type=jnp....  20 us
  transfers between devices with their start and end apart: 13, of which 13 were waited for; matrix products, arithmetic and copies ran while one was open for 7% of the time, Pallas kernels for 0%

commit v1 on v0

v1 whole, which is shorter than its diff:
```python
import functools
import math

import jax
import jax.numpy as jnp
from jax import lax
from jax.experimental import pallas as pl
from jax.experimental.pallas import tpu as pltpu
from jax.sharding import Mesh
from jax.sharding import PartitionSpec as P

HEAD = 128
SHARERS = 8
PER = 4
TILE = 256
BF = jnp.bfloat16
F32 = jnp.float32
I32 = jnp.int32
NT = (((1,), (1,)), ((), ()))


def dot(a, b, dims=(((1,), (0,)), ((), ()))):
    return lax.dot_general(a, b, dims, preferred_element_type=F32)


def pack_kernel(places_ref, q_ref, k_ref, v_ref, g_ref, out_ref):
    n, cap2, rows = out_ref.shape[0], out_ref.shape[1] // (PER + 1), q_ref.shape[0]
    slots = n * cap2
    pick = (places_ref[...] == lax.broadcasted_iota(I32, (slots, 2 * rows), 1)).astype(BF)

    def put(pair, block):
        out_ref[:, pair * cap2 : (pair + 1) * cap2, :] = block.reshape(n, cap2, HEAD).astype(BF)

    for pair in range(0, PER, 2):
        lanes = slice(pair * HEAD, (pair + 2) * HEAD)
        both = dot(pick, jnp.concatenate([q_ref[:, lanes], g_ref[:, lanes]], axis=0))
        put(pair, both[:, :HEAD])
        put(pair + 1, both[:, HEAD:])
    put(PER, dot(pick, jnp.concatenate([k_ref[...], v_ref[...]], axis=0)))


def attend_kernel(
    lens_ref, rows_of_ref, lanes_of_ref, in_ref, out_ref,
    q_s, g_s, k_s, v_s, kt_s, dqt_s, dk_s, dv_s,
):
    groups, rows = lanes_of_ref.shape
    n = in_ref.shape[0] // groups
    cap2 = in_ref.shape[1] // (PER + 1)
    cap = cap2 // 2
    slots = n * cap2
    column = groups * rows
    scale = 1.0 / math.sqrt(HEAD)
    log_scale = scale * math.log2(math.e)

    for group in range(groups):
        want = rows_of_ref[:, group : group + 1]
        want = jnp.concatenate([want, want + cap], axis=0)
        pick = (want == lax.broadcasted_iota(I32, (2 * rows, slots), 1)).astype(BF)
        at = slice(group * rows, (group + 1) * rows)
        here = slice(group * n, (group + 1) * n)

        def got(pair):
            return in_ref[here, pair * cap2 : (pair + 1) * cap2, :].reshape(slots, HEAD)

        for pair in range(0, PER, 2):
            both = dot(pick, jnp.concatenate([got(pair), got(pair + 1)], axis=1)).astype(BF)
            q_s[pair, at, :] = both[:rows, :HEAD]
            q_s[pair + 1, at, :] = both[:rows, HEAD:]
            g_s[pair, at, :] = both[rows:, :HEAD]
            g_s[pair + 1, at, :] = both[rows:, HEAD:]
        both = dot(pick, got(PER))
        k_s[at, :] = both[:rows].astype(BF)
        v_s[at, :] = both[rows:].astype(BF)
        kt_s[:, at] = both[:rows].T.astype(BF)

    dk_s[...] = jnp.zeros_like(dk_s)
    dv_s[...] = jnp.zeros_like(dv_s)

    def head_turn(head, carry):
        for tile in range(column // TILE):
            at = slice(tile * TILE, (tile + 1) * TILE)
            seen = (tile + 1) * TILE
            query = q_s[head, at, :]
            grad = g_s[head, at, :]
            place = lax.broadcasted_iota(I32, (1, TILE), 1) + tile * TILE
            begin = jnp.zeros((1, TILE), I32)
            end = jnp.int32(0)
            for j in range(lens_ref.shape[0]):
                end = end + lens_ref[j]
                begin = jnp.where(end <= place, end, begin)
            key_place = lax.broadcasted_iota(I32, (seen, TILE), 0)
            allowed = (key_place >= begin) & (key_place <= place)
            raw = dot(k_s[:seen, :], query, NT)
            raw = jnp.where(allowed, raw, -1e30)
            top = jnp.max(raw, axis=0, keepdims=True)
            shifted = jnp.exp2((raw - top) * log_scale)
            total = jnp.sum(shifted, axis=0, keepdims=True)
            weights = (shifted * (1.0 / total)).astype(BF)
            d_weights = dot(v_s[:seen, :], grad, NT)
            weights_f = weights.astype(F32)
            product = weights_f * d_weights
            delta = jnp.sum(product, axis=0, keepdims=True)
            dscore = (product - weights_f * delta).astype(BF)
            dqt_s[head, :, at] = (dot(kt_s[:, :seen], dscore) * scale).astype(BF)
            dk_s[:seen, :] += dot(dscore, query)
            dv_s[:seen, :] += dot(weights, grad)
        return carry

    lax.fori_loop(0, PER, head_turn, 0)
    dk_b = (dk_s[...] * scale).astype(BF)
    dv_b = dv_s[...].astype(BF)

    for group in range(groups):
        at = slice(group * rows, (group + 1) * rows)
        here = slice(group * n, (group + 1) * n)
        want = lanes_of_ref[group : group + 1, :]
        want = jnp.concatenate([want, want + cap], axis=1)
        drop = (lax.broadcasted_iota(I32, (slots, 2 * rows), 0) == want).astype(BF)

        def put(pair, block):
            out_ref[here, pair * cap2 : (pair + 1) * cap2, :] = block.reshape(n, cap2, HEAD).astype(BF)

        for pair in range(PER // 2):
            put(
                pair,
                dot(
                    drop,
                    jnp.concatenate([dqt_s[2 * pair, :, at], dqt_s[2 * pair + 1, :, at]], axis=1),
                    NT,
                ),
            )
        put(PER // 2, dot(drop, jnp.concatenate([dk_b[at], dv_b[at]], axis=0)))


def settle_kernel(places_ref, in_ref, q_ref, k_ref, v_ref):
    n, cap2, rows = in_ref.shape[0], in_ref.shape[1] // 3, q_ref.shape[0]
    slots = n * cap2
    pick = (places_ref[...] == lax.broadcasted_iota(I32, (2 * rows, slots), 0)).astype(BF)

    def got(pair):
        return in_ref[:, pair * cap2 : (pair + 1) * cap2, :].reshape(slots, HEAD)

    first = dot(pick, jnp.concatenate([got(0), got(1)], axis=1)).astype(BF)
    q_ref[:, :HEAD] = first[:rows, :HEAD]
    q_ref[:, HEAD : 2 * HEAD] = first[rows:, :HEAD]
    q_ref[:, 2 * HEAD : 3 * HEAD] = first[:rows, HEAD:]
    q_ref[:, 3 * HEAD :] = first[rows:, HEAD:]
    last = dot(pick, got(2)).astype(BF)
    k_ref[...] = last[:rows]
    v_ref[...] = last[rows:]


def body(q_rows, k_rows, value_rows, grad_out, lengths, send_rows, recv_slots):
    rows = q_rows.shape[0]
    plan = send_rows[0]
    n, cap = plan.shape
    slots = 2 * n * cap
    column = SHARERS * rows
    params = pltpu.CompilerParams(vmem_limit_bytes=60 * 1024 * 1024)
    both_halves = jnp.concatenate([plan, jnp.where(plan >= 0, plan + rows, -1)], axis=1)

    slot_list = lax.all_gather(recv_slots[0], "gl", axis=0)
    lanes_of = slot_list // cap * (2 * cap) + slot_list % cap
    own_lengths = lengths[0][lax.axis_index("gh")]

    wide = pl.BlockSpec((rows, PER * HEAD), lambda i: (0, i))
    narrow = pl.BlockSpec((rows, HEAD), lambda i: (0, i))
    packed = pl.pallas_call(
        pack_kernel,
        grid=(SHARERS,),
        in_specs=[pl.BlockSpec((slots, 1), lambda i: (0, 0)), wide, narrow, narrow, wide],
        out_specs=pl.BlockSpec((n, (PER + 1) * 2 * cap, HEAD), lambda i: (i, 0, 0)),
        out_shape=jax.ShapeDtypeStruct((SHARERS * n, (PER + 1) * 2 * cap, HEAD), BF),
        compiler_params=params,
        name="pack",
    )(both_halves.reshape(slots, 1), q_rows, k_rows, value_rows, grad_out)
    arrived = lax.all_to_all(packed, ("gl", "dp"), split_axis=0, concat_axis=0, tiled=True)

    vmem = pl.BlockSpec(memory_space=pltpu.VMEM)
    returned = pl.pallas_call(
        attend_kernel,
        in_specs=[pl.BlockSpec(memory_space=pltpu.SMEM), vmem, vmem, vmem],
        out_specs=vmem,
        out_shape=jax.ShapeDtypeStruct((SHARERS * n, 6 * cap, HEAD), BF),
        scratch_shapes=[
            pltpu.VMEM((PER, column, HEAD), BF),
            pltpu.VMEM((PER, column, HEAD), BF),
            pltpu.VMEM((column, HEAD), BF),
            pltpu.VMEM((column, HEAD), BF),
            pltpu.VMEM((HEAD, column), BF),
            pltpu.VMEM((PER, HEAD, column), BF),
            pltpu.VMEM((column, HEAD), F32),
            pltpu.VMEM((column, HEAD), F32),
        ],
        compiler_params=params,
        name="attend",
    )(own_lengths, lanes_of.T, lanes_of, arrived)
    home = lax.all_to_all(returned, ("gl", "dp"), split_axis=0, concat_axis=0, tiled=True)

    return pl.pallas_call(
        settle_kernel,
        grid=(SHARERS,),
        in_specs=[
            pl.BlockSpec((1, slots), lambda i: (0, 0)),
            pl.BlockSpec((n, 6 * cap, HEAD), lambda i: (i, 0, 0)),
        ],
        out_specs=[wide, narrow, narrow],
        out_shape=[
            jax.ShapeDtypeStruct(q_rows.shape, BF),
            jax.ShapeDtypeStruct(k_rows.shape, BF),
            jax.ShapeDtypeStruct(value_rows.shape, BF),
        ],
        compiler_params=params,
        name="settle",
    )(both_halves.reshape(1, slots), home)


def solution(mesh):
    fine = Mesh(mesh.devices.reshape(-1, SHARERS, mesh.devices.shape[1]), ("gh", "gl", "dp"))
    grp = ("gh", "gl")
    rows = P(("gh", "gl", "dp"), None)
    mapped = jax.shard_map(
        body,
        mesh=fine,
        in_specs=(
            rows,
            rows,
            rows,
            rows,
            P("dp", None, None),
            P(("gh", "gl", "dp"), None, None),
            P("dp", grp),
        ),
        out_specs=(rows, rows, rows),
        check_vma=False,
    )
    return lambda *args: tuple(mapped(*args))
```

time: 566 us -> 210 us (0.37)
  waiting for transfers between devices: 263 us -> 132 us
  local copies, waits for them, and re-layouts: 83 us -> 4.88 us
  matrix products: 66.4 us -> 0 us
  starting transfers between devices: 67.8 us -> 20.5 us
  loops' own time: 42 us -> 0 us
  other arithmetic: 37.9 us -> 1.33 us
  Pallas kernels: 0 us -> 33.2 us
  blocking collectives: 0 us -> 16.2 us
    ppermute x6 -> x0, waiting for transfers between devices: 94.6 us -> none  [from_partner(): return lax.ppermute(value, axis, pairs)]
    dot_general x48 -> x0, matrix products: 66.4 us -> none  [the longest x8 20 us: backward_turn(): jnp.einsum('mk,md->kd', weights_b, grad_part, preferred_element_type=jnp....]
    another operation x2 -> x0, loops' own time: 42 us -> none  [the longest x1 21.1 us: body(): results = lax.map(backward_turn, (indices, saved[0], saved[1:]))]
    all_to_all x7 -> x2, waiting for transfers between devices: 168 us -> 132 us  [the longest x1 74.1 us: body(): lax.all_to_all(packed, ('gl', 'dp'), split_axis=0, concat_axis=0, tiled=T...]
    pallas_call x0 -> x3, Pallas kernels: none -> 33.2 us  [the longest x1 19.2 us: body(): pl.pallas_call(attend_kernel, in_specs=[pl.BlockSpec(memory_space=pltpu.S...]
    all_to_all x7 -> x2, starting transfers between devices: 46.4 us -> 20.5 us  [the longest x1 14.8 us: body(): lax.all_to_all(packed, ('gl', 'dp'), split_axis=0, concat_axis=0, tiled=T...]
    reshape x20 -> x2, local copies, waits for them, and re-layouts: 26.6 us -> 1.45 us  [the longest x1 0.8 us: body(): both_halves.reshape(slots, 1)]
    ppermute x6 -> x0, starting transfers between devices: 21.4 us -> none  [from_partner(): return lax.ppermute(value, axis, pairs)]
  transfers between devices with their start and end apart: 13 -> 2, of which waited for: 13 -> 2; matrix products, arithmetic and copies ran while one was open for 7% -> 1% of each run, Pallas kernels for 0% -> 0%
where the time goes in v1:
time: 210 us; the launch traced here: 209 us
  waiting for transfers between devices  132 us (63%)
  Pallas kernels  33.2 us (16%)
  starting transfers between devices  20.5 us (10%)
  blocking collectives  16.2 us (8%)
  local copies, waits for them, and re-layouts  4.88 us (2%)
    all_to_all x1, waiting for transfers between devices, body(): lax.all_to_all(packed, ('gl', 'dp'), split_axis=0, concat_axis=0, tiled=T...  74.1 us
    all_to_all x1, waiting for transfers between devices, body(): lax.all_to_all(returned, ('gl', 'dp'), split_axis=0, concat_axis=0, tiled...  58.2 us
    pallas_call x1, Pallas kernels, body(): pl.pallas_call(attend_kernel, in_specs=[pl.BlockSpec(memory_space=pltpu.S...  19.2 us
    all_gather x1, blocking collectives, body(): slot_list = lax.all_gather(recv_slots[0], 'gl', axis=0)  16.2 us
    all_to_all x1, starting transfers between devices, body(): lax.all_to_all(packed, ('gl', 'dp'), split_axis=0, concat_axis=0, tiled=T...  14.8 us
    pallas_call x1, Pallas kernels, body(): pl.pallas_call(pack_kernel, grid=(SHARERS,), in_specs=[pl.BlockSpec((slot...  7.61 us
    pallas_call x1, Pallas kernels, body(): pl.pallas_call(settle_kernel, grid=(SHARERS,), in_specs=[pl.BlockSpec((1,...  6.47 us
    all_to_all x1, starting transfers between devices, body(): lax.all_to_all(returned, ('gl', 'dp'), split_axis=0, concat_axis=0, tiled...  5.78 us
  transfers between devices with their start and end apart: 2, of which 2 were waited for; matrix products, arithmetic and copies ran while one was open for 1% of the time, Pallas kernels for 0%

profile of v1, /device:TPU:1, one launch (start us, length us, event | category | flops | bytes accessed | tf_op | source)
XLA Modules:
  0.0 209.2 jit_solution(17372557528039411342)
XLA Ops:
  0.6 0.0 copy-start
  0.6 0.7 add_select_fusion
  1.3 0.7 copy.30
  2.0 0.1 copy.19
  2.1 0.8 reshape.25.places_ref
  2.9 7.6 %pack.1 = bf16[128,120,128]{2,1,0:T(8,128)(2,1)} custom-call(s32[384,1]{1,0:T(8,128)} %reshape.25.places_ref, bf16[128,4096]{1,0:T(8,128)(2,1)} %q_ref.1, bf16[128,1024]{1,0:T(8,128)(2,1)} %k_ref.1, bf16[128,1024]{1,0:T(8,128)(2,1)} %v_ref.1, bf16[128,4096]{1,0:T(8,128)(2,1)} %g_ref.1), custom_call_target="tpu_custom_call" | custom-call | tf_op jit(solution)/shard_map/pack/pallas_call | solution.py:168
  10.5 0.0 copy-start.2
  10.5 14.8 %all-to-all-start = ((bf16[128,120,128]{2,1,0:T(8,128)(2,1)}), bf16[128,120,128]{2,1,0:T(8,128)(2,1)}, u32[]{:S(2)}, u32[]{:S(2)}) async-start(bf16[128,120,128]{2,1,0:T(8,128)(2,1)} %pack.1), calls=%async_computation | async-start | bytes 7864320 | tf_op jit(solution)/shard_map/all_to_all | solution.py:177
  25.3 0.0 copy-done.2
  25.3 16.2 %all-gather = s32[8,1,128]{2,1,0:T(1,128)S(1)} all-gather(s32[1,1,128]{2,1,0:T(1,128)S(1)} %bitcast.38), channel_id=1, replica_groups=mesh['gh'=4,'gl'=8,'dp'=16] {'gl'}, dimensions={0}, use_global_device_ids=true | all-gather | bytes 4608 | tf_op jit(solution)/shard_map/all_gather | solution.py:162
  41.5 0.7 copy.25.rows_of_ref
  42.2 0.0 copy-done
  42.2 0.5 dynamic-slice_bitcast_fusion.lens_ref
  42.8 0.6 fusion.1.lanes_of_ref
  43.4 74.1 %all-to-all-done.in_ref = bf16[128,120,128]{2,1,0:T(8,128)(2,1)} async-done(((bf16[128,120,128]{2,1,0:T(8,128)(2,1)}), bf16[128,120,128]{2,1,0:T(8,128)(2,1)}, u32[]{:S(2)}, u32[]{:S(2)}) %all-to-all-start) | async-done | bytes 3932192 | tf_op jit(solution)/shard_map/all_to_all | solution.py:177
  117.5 19.2 %attend.1 = bf16[128,72,128]{2,1,0:T(8,128)(2,1)} custom-call(s32[4]{0:T(128)} %dynamic-slice_bitcast_fusion.lens_ref, s32[128,8]{1,0:T(8,128)} %copy.25.rows_of_ref, s32[8,128]{1,0:T(8,128)} %fusion.1.lanes_of_ref, bf16[128,120,128]{2,1,0:T(8,128)(2,1)} %all-to-all-done.in_ref), custom_call_target="tpu_custom_call" | custom-call | tf_op jit(solution)/shard_map/attend/pallas_call | solution.py:180
  136.7 5.8 %all-to-all-start.1 = ((bf16[128,72,128]{2,1,0:T(8,128)(2,1)}), bf16[128,72,128]{2,1,0:T(8,128)(2,1)S(1)}, u32[]{:S(2)}, u32[]{:S(2)}) async-start(bf16[128,72,128]{2,1,0:T(8,128)(2,1)} %attend.1), calls=%async_computation.1 | async-start | bytes 4718592 | tf_op jit(solution)/shard_map/all_to_all | solution.py:198
  142.4 0.7 reshape.14.places_ref
  143.1 58.2 %all-to-all-done.1.in_ref = bf16[128,72,128]{2,1,0:T(8,128)(2,1)S(1)} async-done(((bf16[128,72,128]{2,1,0:T(8,128)(2,1)}), bf16[128,72,128]{2,1,0:T(8,128)(2,1)S(1)}, u32[]{:S(2)}, u32[]{:S(2)}) %all-to-all-start.1) | async-done | bytes 2359328 | tf_op jit(solution)/shard_map/all_to_all | solution.py:198
  201.3 0.0 copy-start.1
  201.3 1.4 copy-done.1
  202.7 6.5 %settle.1 = (bf16[128,4096]{1,0:T(8,128)(2,1)}, bf16[128,1024]{1,0:T(8,128)(2,1)}, bf16[128,1024]{1,0:T(8,128)(2,1)}) custom-call(s32[1,384]{1,0:T(1,128)} %reshape.14.places_ref, bf16[128,72,128]{2,1,0:T(8,128)(2,1)} %copy-done.1), custom_call_target="tpu_custom_call" | custom-call | tf_op jit(solution)/shard_map/settle/pallas_call | solution.py:200
  (2 shorter events, 0.0 us)
Async XLA Ops:
  0.6 41.6 %copy-start = (s32[1,4,4]{2,1,0:T(4,128)S(1)}, s32[1,4,4]{2,1,0:T(4,128)}, u32[]{:S(2)}) copy-start(s32[1,4,4]{2,1,0:T(4,128)} %param.11) | copy-start | bytes 196
  10.5 14.8 %copy-start.2 = (s32[1,128]{1,0:T(1,128)S(1)}, s32[1,128]{1,0:T(1,128)}, u32[]{:S(2)}) copy-start(s32[1,128]{1,0:T(1,128)} %param.13) | copy-start | bytes 1540
  10.5 106.9 %all-to-all-start = ((bf16[128,120,128]{2,1,0:T(8,128)(2,1)}), bf16[128,120,128]{2,1,0:T(8,128)(2,1)}, u32[]{:S(2)}, u32[]{:S(2)}) async-start(bf16[128,120,128]{2,1,0:T(8,128)(2,1)} %pack.1), calls=%async_computation | async-start | bytes 7864320 | tf_op jit(solution)/shard_map/all_to_all | solution.py:177
  136.7 64.7 %all-to-all-start.1 = ((bf16[128,72,128]{2,1,0:T(8,128)(2,1)}), bf16[128,72,128]{2,1,0:T(8,128)(2,1)S(1)}, u32[]{:S(2)}, u32[]{:S(2)}) async-start(bf16[128,72,128]{2,1,0:T(8,128)(2,1)} %attend.1), calls=%async_computation.1 | async-start | bytes 4718592 | tf_op jit(solution)/shard_map/all_to_all | solution.py:198
  201.3 1.4 copy-start.1

commit v2 on v1

v2 whole, which is shorter than its diff:
```python
import math

import jax
import jax.numpy as jnp
from jax import lax
from jax.experimental import pallas as pl
from jax.experimental.pallas import tpu as pltpu
from jax.sharding import Mesh
from jax.sharding import PartitionSpec as P

HEAD = 128
SHARERS = 8
LOW = -1e30
PER = 4
TILE = 256
BF = jnp.bfloat16
F32 = jnp.float32
I32 = jnp.int32
NT = (((1,), (1,)), ((), ()))


def dot(a, b, dims=(((1,), (0,)), ((), ()))):
    return lax.dot_general(a, b, dims, preferred_element_type=F32)


def spread(plan, rows):
    n, cap = plan.shape
    cap2 = 2 * cap
    slots = n * cap2
    both = jnp.concatenate([plan, jnp.where(plan >= 0, plan + rows, -1)], axis=1)
    slot = lax.broadcasted_iota(I32, (slots, n), 0)
    first = lax.broadcasted_iota(I32, (slots, n), 1) * cap2
    owns = (slot >= first) & (slot < first + cap2)
    table = dot(owns.astype(BF), both.astype(F32).astype(BF))
    base = jnp.sum(jnp.where(owns, first, 0), axis=1, keepdims=True)
    within = lax.broadcasted_iota(I32, (slots, cap2), 0) - base
    here = within == lax.broadcasted_iota(I32, (slots, cap2), 1)
    return jnp.sum(jnp.where(here, table, 0.0), axis=1, keepdims=True)


def pack_kernel(
    plan_ref, q_hbm, k_hbm, v_hbm, g_hbm, out_ref, q_s, k_s, v_s, g_s, sems
):
    n, cap = plan_ref.shape
    rows = q_s.shape[0]
    cap2 = 2 * cap
    slots = n * cap2
    pairs = ((q_hbm, q_s), (k_hbm, k_s), (v_hbm, v_s), (g_hbm, g_s))
    copies = []
    for group in range(SHARERS):
        for i, (source, held) in enumerate(pairs):
            width = held.shape[1] // SHARERS
            lanes = pl.ds(group * width, width)
            copies.append(
                pltpu.make_async_copy(source.at[:, lanes], held.at[:, lanes], sems.at[group, i])
            )
            copies[-1].start()
    want = spread(plan_ref[...], rows)
    pick = (want == lax.broadcasted_iota(I32, (slots, 2 * rows), 1).astype(F32)).astype(BF)

    for group in range(SHARERS):
        for copy in copies[group * 4 : group * 4 + 4]:
            copy.wait()

        def put(pair, block):
            out_ref[group * n : (group + 1) * n, pair * cap2 : (pair + 1) * cap2, :] = (
                block.reshape(n, cap2, HEAD).astype(BF)
            )

        for pair in range(0, PER, 2):
            lanes = slice((group * PER + pair) * HEAD, (group * PER + pair + 2) * HEAD)
            both = dot(pick, jnp.concatenate([q_s[:, lanes], g_s[:, lanes]], axis=0))
            put(pair, both[:, :HEAD])
            put(pair + 1, both[:, HEAD:])
        lanes = slice(group * HEAD, (group + 1) * HEAD)
        put(PER, dot(pick, jnp.concatenate([k_s[:, lanes], v_s[:, lanes]], axis=0)))


def attend_kernel(
    lens_ref, rows_of_ref, lanes_of_ref, in_ref, out_ref,
    q_s, g_s, k_s, v_s, kt_s, dqt_s, dk_s, dv_s,
):
    groups, rows = lanes_of_ref.shape
    n = in_ref.shape[0] // groups
    cap2 = in_ref.shape[1] // (PER + 1)
    cap = cap2 // 2
    slots = n * cap2
    column = groups * rows
    scale = 1.0 / math.sqrt(HEAD)
    log_scale = scale * math.log2(math.e)

    for group in range(groups):
        want = rows_of_ref[:, group : group + 1]
        want = jnp.concatenate([want, want + cap], axis=0)
        pick = (want == lax.broadcasted_iota(I32, (2 * rows, slots), 1)).astype(BF)
        at = slice(group * rows, (group + 1) * rows)
        here = slice(group * n, (group + 1) * n)

        def got(pair):
            return in_ref[here, pair * cap2 : (pair + 1) * cap2, :].reshape(slots, HEAD)

        for pair in range(0, PER, 2):
            both = dot(pick, jnp.concatenate([got(pair), got(pair + 1)], axis=1)).astype(BF)
            q_s[pair, at, :] = both[:rows, :HEAD]
            q_s[pair + 1, at, :] = both[:rows, HEAD:]
            g_s[pair, at, :] = both[rows:, :HEAD]
            g_s[pair + 1, at, :] = both[rows:, HEAD:]
        both = dot(pick, got(PER))
        k_s[at, :] = both[:rows].astype(BF)
        v_s[at, :] = both[rows:].astype(BF)
        kt_s[:, at] = both[:rows].T.astype(BF)

    dk_s[...] = jnp.zeros_like(dk_s)
    dv_s[...] = jnp.zeros_like(dv_s)
    key_at = lax.broadcasted_iota(I32, (column, TILE), 0)
    causal = key_at[:TILE] <= lax.broadcasted_iota(I32, (TILE, TILE), 1)

    for tile in range(column // TILE):
        old, seen = tile * TILE, (tile + 1) * TILE
        place = lax.broadcasted_iota(I32, (1, TILE), 1) + old
        begin = jnp.zeros((1, TILE), I32)
        end = jnp.int32(0)
        for j in range(lens_ref.shape[0]):
            end = end + lens_ref[j]
            begin = jnp.where(end <= place, end, begin)

        def masked(raw):
            last = jnp.where((key_at[:TILE] >= begin - old) & causal, raw[old:], LOW)
            if not tile:
                return last
            return jnp.concatenate([jnp.where(key_at[:old] >= begin, raw[:old], LOW), last], axis=0)

        queries = [q_s[head, old:seen, :] for head in range(PER)]
        grads = [g_s[head, old:seen, :] for head in range(PER)]
        raws = [masked(dot(k_s[:seen, :], query, NT)) for query in queries]
        d_weights = [dot(v_s[:seen, :], grad, NT) for grad in grads]
        weights, dscores = [], []
        for head in range(PER):
            top = jnp.max(raws[head], axis=0, keepdims=True)
            shifted = jnp.exp2((raws[head] - top) * log_scale)
            total = jnp.sum(shifted, axis=0, keepdims=True)
            weight = (shifted * (1.0 / total)).astype(BF)
            weight_f = weight.astype(F32)
            delta = jnp.sum(weight_f * d_weights[head], axis=0, keepdims=True)
            dscore = (weight_f * (d_weights[head] - delta)).astype(BF)
            dqt_s[head, :, old:seen] = (dot(kt_s[:, :seen], dscore) * scale).astype(BF)
            weights.append(weight)
            dscores.append(dscore)
        dk_s[:seen, :] += dot(jnp.concatenate(dscores, axis=1), jnp.concatenate(queries, axis=0))
        dv_s[:seen, :] += dot(jnp.concatenate(weights, axis=1), jnp.concatenate(grads, axis=0))

    dk_b = (dk_s[...] * scale).astype(BF)
    dv_b = dv_s[...].astype(BF)

    for group in range(groups):
        at = slice(group * rows, (group + 1) * rows)
        here = slice(group * n, (group + 1) * n)
        want = lanes_of_ref[group : group + 1, :]
        want = jnp.concatenate([want, want + cap], axis=1)
        drop = (lax.broadcasted_iota(I32, (slots, 2 * rows), 0) == want).astype(BF)

        def put(pair, block):
            out_ref[here, pair * cap2 : (pair + 1) * cap2, :] = block.reshape(n, cap2, HEAD).astype(BF)

        for pair in range(PER // 2):
            put(
                pair,
                dot(
                    drop,
                    jnp.concatenate([dqt_s[2 * pair, :, at], dqt_s[2 * pair + 1, :, at]], axis=1),
                    NT,
                ),
            )
        put(PER // 2, dot(drop, jnp.concatenate([dk_b[at], dv_b[at]], axis=0)))


def settle_kernel(places_ref, in_ref, q_hbm, k_hbm, v_hbm, q_s, k_s, v_s, sems):
    n, cap2, rows = in_ref.shape[0] // SHARERS, in_ref.shape[1] // 3, q_s.shape[0]
    slots = n * cap2
    pick = (places_ref[...] == lax.broadcasted_iota(I32, (2 * rows, slots), 0)).astype(BF)
    copies = []
    for group in range(SHARERS):
        here = slice(group * n, (group + 1) * n)

        def got(pair):
            return in_ref[here, pair * cap2 : (pair + 1) * cap2, :].reshape(slots, HEAD)

        first = dot(pick, jnp.concatenate([got(0), got(1)], axis=1)).astype(BF)
        base = group * PER * HEAD
        q_s[:, base : base + HEAD] = first[:rows, :HEAD]
        q_s[:, base + HEAD : base + 2 * HEAD] = first[rows:, :HEAD]
        q_s[:, base + 2 * HEAD : base + 3 * HEAD] = first[:rows, HEAD:]
        q_s[:, base + 3 * HEAD : base + 4 * HEAD] = first[rows:, HEAD:]
        last = dot(pick, got(2)).astype(BF)
        lanes = slice(group * HEAD, (group + 1) * HEAD)
        k_s[:, lanes] = last[:rows]
        v_s[:, lanes] = last[rows:]
        for i, (held, target) in enumerate(((q_s, q_hbm), (k_s, k_hbm), (v_s, v_hbm))):
            width = held.shape[1] // SHARERS
            lanes = pl.ds(group * width, width)
            copies.append(
                pltpu.make_async_copy(held.at[:, lanes], target.at[:, lanes], sems.at[group, i])
            )
            copies[-1].start()
    for copy in copies:
        copy.wait()


VMEM = pl.BlockSpec(memory_space=pltpu.VMEM)
OUTSIDE = pl.BlockSpec(memory_space=pltpu.HBM)


def limit(mib):
    return pltpu.CompilerParams(vmem_limit_bytes=mib * 1024 * 1024)


def pack(plan, q_rows, k_rows, value_rows, grad_out):
    n, cap = plan.shape
    args = (q_rows, k_rows, value_rows, grad_out)
    return pl.pallas_call(
        pack_kernel,
        in_specs=[VMEM] + [OUTSIDE] * 4,
        out_specs=VMEM,
        out_shape=pltpu.VMEM((SHARERS * n, (PER + 1) * 2 * cap, HEAD), BF),
        scratch_shapes=[pltpu.VMEM(a.shape, BF) for a in args]
        + [pltpu.SemaphoreType.DMA((SHARERS, 4))],
        compiler_params=limit(16),
        name="pack",
    )(plan, *(pltpu.with_memory_space_constraint(a, pltpu.HBM) for a in args))


def attend(own_lengths, slot_list, arrived, cap):
    lanes_of = slot_list // cap * (2 * cap) + slot_list % cap
    column = slot_list.size
    return pl.pallas_call(
        attend_kernel,
        in_specs=[pl.BlockSpec(memory_space=pltpu.SMEM), VMEM, VMEM, VMEM],
        out_specs=VMEM,
        out_shape=pltpu.VMEM((arrived.shape[0], 6 * cap, HEAD), BF),
        scratch_shapes=[
            pltpu.VMEM((PER, column, HEAD), BF),
            pltpu.VMEM((PER, column, HEAD), BF),
            pltpu.VMEM((column, HEAD), BF),
            pltpu.VMEM((column, HEAD), BF),
            pltpu.VMEM((HEAD, column), BF),
            pltpu.VMEM((PER, HEAD, column), BF),
            pltpu.VMEM((column, HEAD), F32),
            pltpu.VMEM((column, HEAD), F32),
        ],
        compiler_params=limit(32),
        name="attend",
    )(own_lengths, lanes_of.T, lanes_of, pltpu.with_memory_space_constraint(arrived, pltpu.VMEM))


def settle(plan, rows, home):
    n, cap = plan.shape
    both_halves = jnp.concatenate([plan, jnp.where(plan >= 0, plan + rows, -1)], axis=1)
    outs = [
        jax.ShapeDtypeStruct((rows, SHARERS * width * HEAD), BF) for width in (PER, 1, 1)
    ]
    return pl.pallas_call(
        settle_kernel,
        in_specs=[VMEM, VMEM],
        out_specs=[OUTSIDE] * 3,
        out_shape=outs,
        scratch_shapes=[pltpu.VMEM(a.shape, BF) for a in outs]
        + [pltpu.SemaphoreType.DMA((SHARERS, 3))],
        compiler_params=limit(16),
        name="settle",
    )(both_halves.reshape(1, -1), pltpu.with_memory_space_constraint(home, pltpu.VMEM))


def exchange(bundle):
    return lax.all_to_all(bundle, ("gl", "dp"), split_axis=0, concat_axis=0, tiled=True)


def body(q_rows, k_rows, value_rows, grad_out, lengths, send_rows, recv_slots):
    plan = send_rows[0]
    cap = plan.shape[1]
    slot_list = lax.all_gather(recv_slots[0], "gl", axis=0)
    own_lengths = lengths[0][lax.axis_index("gh")]
    arrived = exchange(pack(plan, q_rows, k_rows, value_rows, grad_out))
    home = exchange(attend(own_lengths, slot_list, arrived, cap))
    return settle(plan, q_rows.shape[0], home)


def solution(mesh):
    fine = Mesh(mesh.devices.reshape(-1, SHARERS, mesh.devices.shape[1]), ("gh", "gl", "dp"))
    grp = ("gh", "gl")
    rows = P(("gh", "gl", "dp"), None)
    mapped = jax.shard_map(
        body,
        mesh=fine,
        in_specs=(
            rows,
            rows,
            rows,
            rows,
            P("dp", None, None),
            P(("gh", "gl", "dp"), None, None),
            P("dp", grp),
        ),
        out_specs=(rows, rows, rows),
        check_vma=False,
    )
    return lambda *args: tuple(mapped(*args))
```

time: 210 us -> 199 us (0.948)
  Pallas kernels: 33.2 us -> 21.5 us
  waiting for transfers between devices: 132 us -> 135 us
    pallas_call x3, Pallas kernels: 33.2 us -> 21.5 us  [the longest x1 15.3 us: attend(): pl.pallas_call(attend_kernel, in_specs=[pl.BlockSpec(memory_space=pltpu.S...]
    all_to_all x2, waiting for transfers between devices: 132 us -> 135 us  [exchange(): lax.all_to_all(bundle, ('gl', 'dp'), split_axis=0, concat_axis=0, tiled=T...]
  transfers between devices with their start and end apart: 2 -> 2, of which waited for: 2 -> 2; matrix products, arithmetic and copies ran while one was open for 1% -> 0% of each run, Pallas kernels for 0% -> 0%
where the time goes in v2:
time: 199 us; the launch traced here: 198 us
  waiting for transfers between devices  135 us (68%)
  Pallas kernels  21.5 us (11%)
  starting transfers between devices  20.7 us (10%)
  blocking collectives  16.2 us (8%)
  local copies, waits for them, and re-layouts  4.26 us (2%)
    all_to_all x2, waiting for transfers between devices, exchange(): lax.all_to_all(bundle, ('gl', 'dp'), split_axis=0, concat_axis=0, tiled=T...  135 us
    all_to_all x2, starting transfers between devices, exchange(): lax.all_to_all(bundle, ('gl', 'dp'), split_axis=0, concat_axis=0, tiled=T...  20.7 us
    all_gather x1, blocking collectives, body(): slot_list = lax.all_gather(recv_slots[0], 'gl', axis=0)  16.2 us
    pallas_call x1, Pallas kernels, attend(): pl.pallas_call(attend_kernel, in_specs=[pl.BlockSpec(memory_space=pltpu.S...  15.3 us
    pallas_call x1, Pallas kernels, pack(): pl.pallas_call(pack_kernel, in_specs=[VMEM] + [OUTSIDE] * 4, out_specs=VM...  4.23 us
    unnamed x9, local copies, waits for them, and re-layouts  4.05 us
  transfers between devices with their start and end apart: 2, of which 2 were waited for; matrix products, arithmetic and copies ran while one was open for 0% of the time, Pallas kernels for 0%

profile of v2, /device:TPU:1, one launch (start us, length us, event | category | flops | bytes accessed | tf_op | source)
XLA Modules:
  0.0 198.2 jit_solution(3178538301991742231)
XLA Ops:
  0.6 0.0 copy-start
  0.6 0.8 copy.13
  1.4 4.2 %pack.1 = bf16[128,120,128]{2,1,0:T(8,128)(2,1)S(1)} custom-call(s32[16,12]{1,0:T(8,128)S(1)} %bitcast.32, bf16[128,4096]{1,0:T(8,128)(2,1)} %q_hbm.1, bf16[128,1024]{1,0:T(8,128)(2,1)} %k_hbm.1, bf16[128,1024]{1,0:T(8,128)(2,1)} %v_hbm.1, bf16[128,4096]{1,0:T(8,128)(2,1)} %g_hbm.1), custom_call_target="tpu_custom_call" | custom-call | tf_op jit(solution)/shard_map/pack/pallas_call | solution.py:220
  5.7 0.0 copy-start.1
  5.7 1.9 copy-done.1
  7.5 0.0 copy-start.3
  7.5 14.7 %all-to-all-start = ((bf16[128,120,128]{2,1,0:T(8,128)(2,1)}), bf16[128,120,128]{2,1,0:T(8,128)(2,1)}, u32[]{:S(2)}, u32[]{:S(2)}) async-start(bf16[128,120,128]{2,1,0:T(8,128)(2,1)} %copy-done.1), calls=%async_computation | async-start | bytes 7864320 | tf_op jit(solution)/shard_map/all_to_all | solution.py:274
  22.3 0.0 copy-done.3
  22.3 16.2 %all-gather = s32[8,1,128]{2,1,0:T(1,128)S(1)} all-gather(s32[1,1,128]{2,1,0:T(1,128)S(1)} %bitcast.36), channel_id=1, replica_groups=mesh['gh'=4,'gl'=8,'dp'=16] {'gl'}, dimensions={0}, use_global_device_ids=true | all-gather | bytes 4608 | tf_op jit(solution)/shard_map/all_gather | solution.py:280
  38.5 0.1 copy.17.rows_of_ref
  38.6 0.0 copy-done
  38.7 75.8 %all-to-all-done.in_ref = bf16[128,120,128]{2,1,0:T(8,128)(2,1)} async-done(((bf16[128,120,128]{2,1,0:T(8,128)(2,1)}), bf16[128,120,128]{2,1,0:T(8,128)(2,1)}, u32[]{:S(2)}, u32[]{:S(2)}) %all-to-all-start) | async-done | bytes 3932192 | tf_op jit(solution)/shard_map/all_to_all | solution.py:274
  114.5 15.3 %attend.1 = bf16[128,72,128]{2,1,0:T(8,128)(2,1)S(1)} custom-call(s32[4]{0:T(128)S(1)} %dynamic-slice_bitcast_fusion.lens_ref, s32[128,8]{1,0:T(8,128)S(1)} %copy.17.rows_of_ref, s32[8,128]{1,0:T(8,128)S(1)} %fusion.1.lanes_of_ref, bf16[128,120,128]{2,1,0:T(8,128)(2,1)} %all-to-all-done.in_ref), custom_call_target="tpu_custom_call" | custom-call | tf_op jit(solution)/shard_map/attend/pallas_call | solution.py:235
  129.8 0.0 copy-start.2
  129.8 1.4 copy-done.2
  131.2 6.0 %all-to-all-start.1 = ((bf16[128,72,128]{2,1,0:T(8,128)(2,1)}), bf16[128,72,128]{2,1,0:T(8,128)(2,1)S(1)}, u32[]{:S(2)}, u32[]{:S(2)}) async-start(bf16[128,72,128]{2,1,0:T(8,128)(2,1)} %copy-done.2), calls=%async_computation.1 | async-start | bytes 4718592 | tf_op jit(solution)/shard_map/all_to_all | solution.py:274
  137.2 0.1 pad_add_fusion
  137.3 0.1 reshape.11.places_ref
  137.4 58.7 %all-to-all-done.1.in_ref = bf16[128,72,128]{2,1,0:T(8,128)(2,1)S(1)} async-done(((bf16[128,72,128]{2,1,0:T(8,128)(2,1)}), bf16[128,72,128]{2,1,0:T(8,128)(2,1)S(1)}, u32[]{:S(2)}, u32[]{:S(2)}) %all-to-all-start.1) | async-done | bytes 2359328 | tf_op jit(solution)/shard_map/all_to_all | solution.py:274
  196.0 2.0 %settle.1 = (bf16[128,4096]{1,0:T(8,128)(2,1)}, bf16[128,1024]{1,0:T(8,128)(2,1)}, bf16[128,1024]{1,0:T(8,128)(2,1)}) custom-call(s32[1,384]{1,0:T(1,128)S(1)} %reshape.11.places_ref, bf16[128,72,128]{2,1,0:T(8,128)(2,1)S(1)} %all-to-all-done.1.in_ref), custom_call_target="tpu_custom_call" | custom-call | tf_op jit(solution)/shard_map/settle/pallas_call | solution.py:261
  (4 shorter events, 0.0 us)
Async XLA Ops:
  0.6 38.0 %copy-start = (s32[1,4,4]{2,1,0:T(4,128)S(1)}, s32[1,4,4]{2,1,0:T(4,128)}, u32[]{:S(2)}) copy-start(s32[1,4,4]{2,1,0:T(4,128)} %param.11) | copy-start | bytes 196
  5.7 1.9 copy-start.1
  7.5 14.8 %copy-start.3 = (s32[1,128]{1,0:T(1,128)S(1)}, s32[1,128]{1,0:T(1,128)}, u32[]{:S(2)}) copy-start(s32[1,128]{1,0:T(1,128)} %param.13) | copy-start | bytes 1540
  7.5 106.9 %all-to-all-start = ((bf16[128,120,128]{2,1,0:T(8,128)(2,1)}), bf16[128,120,128]{2,1,0:T(8,128)(2,1)}, u32[]{:S(2)}, u32[]{:S(2)}) async-start(bf16[128,120,128]{2,1,0:T(8,128)(2,1)} %copy-done.1), calls=%async_computation | async-start | bytes 7864320 | tf_op jit(solution)/shard_map/all_to_all | solution.py:274
  129.8 1.4 copy-start.2
  131.2 64.9 %all-to-all-start.1 = ((bf16[128,72,128]{2,1,0:T(8,128)(2,1)}), bf16[128,72,128]{2,1,0:T(8,128)(2,1)S(1)}, u32[]{:S(2)}, u32[]{:S(2)}) async-start(bf16[128,72,128]{2,1,0:T(8,128)(2,1)} %copy-done.2), calls=%async_computation.1 | async-start | bytes 4718592 | tf_op jit(solution)/shard_map/all_to_all | solution.py:274

commit v3 on v2

--- a/solution.py
+++ b/solution.py
@@ -10,6 +10,7 @@
 
 HEAD = 128
 SHARERS = 8
+CORES = 2
 LOW = -1e30
 PER = 4
 TILE = 256
@@ -23,25 +24,35 @@
     return lax.dot_general(a, b, dims, preferred_element_type=F32)
 
 
-def spread(plan, rows):
-    n, cap = plan.shape
+def wanted(plan_ref, rows, along_lanes):
+    cap, _, n = plan_ref.shape
     cap2 = 2 * cap
     slots = n * cap2
-    both = jnp.concatenate([plan, jnp.where(plan >= 0, plan + rows, -1)], axis=1)
-    slot = lax.broadcasted_iota(I32, (slots, n), 0)
-    first = lax.broadcasted_iota(I32, (slots, n), 1) * cap2
+    axis = 0 if along_lanes else 1
+
+    def iotas(size):
+        shape = (size, slots) if along_lanes else (slots, size)
+        return lax.broadcasted_iota(I32, shape, axis), lax.broadcasted_iota(I32, shape, 1 - axis)
+
+    target, slot = iotas(n)
+    first = target * cap2
     owns = (slot >= first) & (slot < first + cap2)
-    table = dot(owns.astype(BF), both.astype(F32).astype(BF))
-    base = jnp.sum(jnp.where(owns, first, 0), axis=1, keepdims=True)
-    within = lax.broadcasted_iota(I32, (slots, cap2), 0) - base
-    here = within == lax.broadcasted_iota(I32, (slots, cap2), 1)
-    return jnp.sum(jnp.where(here, table, 0.0), axis=1, keepdims=True)
+    plan = plan_ref[:, 0, :].astype(F32).astype(BF)
+    hot = owns.astype(BF)
+    table = dot(plan, hot) if along_lanes else dot(hot, plan, NT)
+    base = jnp.sum(jnp.where(owns, first, 0), axis=axis, keepdims=True)
+    entry, slot = iotas(cap)
+    within = slot - base
+    chosen = (within == entry) | (within == entry + cap)
+    value = jnp.sum(jnp.where(chosen, table, 0.0), axis=axis, keepdims=True)
+    late = jnp.sum(jnp.where(within == entry + cap, 1.0, 0.0), axis=axis, keepdims=True)
+    return jnp.where(value >= 0.0, value + late * rows, -1.0)
 
 
 def pack_kernel(
-    plan_ref, q_hbm, k_hbm, v_hbm, g_hbm, out_ref, q_s, k_s, v_s, g_s, sems
+    plan_ref, q_hbm, k_hbm, v_hbm, g_hbm, out_hbm, q_s, k_s, v_s, g_s, out_s, sems, out_sems
 ):
-    n, cap = plan_ref.shape
+    cap, _, n = plan_ref.shape
     rows = q_s.shape[0]
     cap2 = 2 * cap
     slots = n * cap2
@@ -55,15 +66,16 @@
                 pltpu.make_async_copy(source.at[:, lanes], held.at[:, lanes], sems.at[group, i])
             )
             copies[-1].start()
-    want = spread(plan_ref[...], rows)
+    want = wanted(plan_ref, rows, False)
     pick = (want == lax.broadcasted_iota(I32, (slots, 2 * rows), 1).astype(F32)).astype(BF)
+    sends = []
 
     for group in range(SHARERS):
         for copy in copies[group * 4 : group * 4 + 4]:
             copy.wait()
 
         def put(pair, block):
-            out_ref[group * n : (group + 1) * n, pair * cap2 : (pair + 1) * cap2, :] = (
+            out_s[group // CORES, :, group % CORES, pair * cap2 : (pair + 1) * cap2, :] = (
                 block.reshape(n, cap2, HEAD).astype(BF)
             )
 
@@ -74,6 +86,13 @@
             put(pair + 1, both[:, HEAD:])
         lanes = slice(group * HEAD, (group + 1) * HEAD)
         put(PER, dot(pick, jnp.concatenate([k_s[:, lanes], v_s[:, lanes]], axis=0)))
+        block = (group // CORES, slice(None), group % CORES)
+        sends.append(
+            pltpu.make_async_copy(out_s.at[block], out_hbm.at[block], out_sems.at[group])
+        )
+        sends[-1].start()
+    for send in sends:
+        send.wait()
 
 
 def attend_kernel(
@@ -81,8 +100,8 @@
     q_s, g_s, k_s, v_s, kt_s, dqt_s, dk_s, dv_s,
 ):
     groups, rows = lanes_of_ref.shape
-    n = in_ref.shape[0] // groups
-    cap2 = in_ref.shape[1] // (PER + 1)
+    n = in_ref.shape[1]
+    cap2 = in_ref.shape[3] // (PER + 1)
     cap = cap2 // 2
     slots = n * cap2
     column = groups * rows
@@ -94,10 +113,10 @@
         want = jnp.concatenate([want, want + cap], axis=0)
         pick = (want == lax.broadcasted_iota(I32, (2 * rows, slots), 1)).astype(BF)
         at = slice(group * rows, (group + 1) * rows)
-        here = slice(group * n, (group + 1) * n)
 
         def got(pair):
-            return in_ref[here, pair * cap2 : (pair + 1) * cap2, :].reshape(slots, HEAD)
+            part = in_ref[group // CORES, :, group % CORES, pair * cap2 : (pair + 1) * cap2, :]
+            return part.reshape(slots, HEAD)
 
         for pair in range(0, PER, 2):
             both = dot(pick, jnp.concatenate([got(pair), got(pair + 1)], axis=1)).astype(BF)
@@ -154,13 +173,14 @@
 
     for group in range(groups):
         at = slice(group * rows, (group + 1) * rows)
-        here = slice(group * n, (group + 1) * n)
         want = lanes_of_ref[group : group + 1, :]
         want = jnp.concatenate([want, want + cap], axis=1)
         drop = (lax.broadcasted_iota(I32, (slots, 2 * rows), 0) == want).astype(BF)
 
         def put(pair, block):
-            out_ref[here, pair * cap2 : (pair + 1) * cap2, :] = block.reshape(n, cap2, HEAD).astype(BF)
+            out_ref[group // CORES, :, group % CORES, pair * cap2 : (pair + 1) * cap2, :] = (
+                block.reshape(n, cap2, HEAD).astype(BF)
+            )
 
         for pair in range(PER // 2):
             put(
@@ -174,16 +194,17 @@
         put(PER // 2, dot(drop, jnp.concatenate([dk_b[at], dv_b[at]], axis=0)))
 
 
-def settle_kernel(places_ref, in_ref, q_hbm, k_hbm, v_hbm, q_s, k_s, v_s, sems):
-    n, cap2, rows = in_ref.shape[0] // SHARERS, in_ref.shape[1] // 3, q_s.shape[0]
+def settle_kernel(plan_ref, in_ref, q_hbm, k_hbm, v_hbm, q_s, k_s, v_s, sems):
+    n, cap2, rows = in_ref.shape[1], in_ref.shape[3] // 3, q_s.shape[0]
     slots = n * cap2
-    pick = (places_ref[...] == lax.broadcasted_iota(I32, (2 * rows, slots), 0)).astype(BF)
+    want = wanted(plan_ref, rows, True)
+    pick = (want == lax.broadcasted_iota(I32, (2 * rows, slots), 0).astype(F32)).astype(BF)
     copies = []
     for group in range(SHARERS):
-        here = slice(group * n, (group + 1) * n)
 
         def got(pair):
-            return in_ref[here, pair * cap2 : (pair + 1) * cap2, :].reshape(slots, HEAD)
+            part = in_ref[group // CORES, :, group % CORES, pair * cap2 : (pair + 1) * cap2, :]
+            return part.reshape(slots, HEAD)
 
         first = dot(pick, jnp.concatenate([got(0), got(1)], axis=1)).astype(BF)
         base = group * PER * HEAD
@@ -215,15 +236,20 @@
 
 
 def pack(plan, q_rows, k_rows, value_rows, grad_out):
-    n, cap = plan.shape
+    cap, _, n = plan.shape
     args = (q_rows, k_rows, value_rows, grad_out)
+    shape = (SHARERS // CORES, n, CORES, (PER + 1) * 2 * cap, HEAD)
     return pl.pallas_call(
         pack_kernel,
         in_specs=[VMEM] + [OUTSIDE] * 4,
-        out_specs=VMEM,
-        out_shape=pltpu.VMEM((SHARERS * n, (PER + 1) * 2 * cap, HEAD), BF),
+        out_specs=OUTSIDE,
+        out_shape=pltpu.HBM(shape, BF),
         scratch_shapes=[pltpu.VMEM(a.shape, BF) for a in args]
-        + [pltpu.SemaphoreType.DMA((SHARERS, 4))],
+        + [
+            pltpu.VMEM(shape, BF),
+            pltpu.SemaphoreType.DMA((SHARERS, 4)),
+            pltpu.SemaphoreType.DMA((SHARERS,)),
+        ],
         compiler_params=limit(16),
         name="pack",
     )(plan, *(pltpu.with_memory_space_constraint(a, pltpu.HBM) for a in args))
@@ -236,7 +262,7 @@
         attend_kernel,
         in_specs=[pl.BlockSpec(memory_space=pltpu.SMEM), VMEM, VMEM, VMEM],
         out_specs=VMEM,
-        out_shape=pltpu.VMEM((arrived.shape[0], 6 * cap, HEAD), BF),
+        out_shape=pltpu.VMEM(arrived.shape[:3] + (6 * cap, HEAD), BF),
         scratch_shapes=[
             pltpu.VMEM((PER, column, HEAD), BF),
             pltpu.VMEM((PER, column, HEAD), BF),
@@ -249,12 +275,10 @@
         ],
         compiler_params=limit(32),
         name="attend",
-    )(own_lengths, lanes_of.T, lanes_of, pltpu.with_memory_space_constraint(arrived, pltpu.VMEM))
+    )(own_lengths, lanes_of.T, lanes_of, arrived)
 
 
 def settle(plan, rows, home):
-    n, cap = plan.shape
-    both_halves = jnp.concatenate([plan, jnp.where(plan >= 0, plan + rows, -1)], axis=1)
     outs = [
         jax.ShapeDtypeStruct((rows, SHARERS * width * HEAD), BF) for width in (PER, 1, 1)
     ]
@@ -267,17 +291,20 @@
         + [pltpu.SemaphoreType.DMA((SHARERS, 3))],
         compiler_params=limit(16),
         name="settle",
-    )(both_halves.reshape(1, -1), pltpu.with_memory_space_constraint(home, pltpu.VMEM))
+    )(plan, pltpu.with_memory_space_constraint(home, pltpu.VMEM))
 
 
 def exchange(bundle):
-    return lax.all_to_all(bundle, ("gl", "dp"), split_axis=0, concat_axis=0, tiled=True)
+    flat = bundle.reshape((-1,) + bundle.shape[3:])
+    return lax.all_to_all(
+        flat, ("zx", "dp", "core"), split_axis=0, concat_axis=0, tiled=True
+    ).reshape(bundle.shape)
 
 
 def body(q_rows, k_rows, value_rows, grad_out, lengths, send_rows, recv_slots):
-    plan = send_rows[0]
-    cap = plan.shape[1]
-    slot_list = lax.all_gather(recv_slots[0], "gl", axis=0)
+    plan = jnp.transpose(send_rows, (2, 0, 1))
+    cap = plan.shape[0]
+    slot_list = lax.all_gather(recv_slots[0], ("zx", "core"), axis=0)
     own_lengths = lengths[0][lax.axis_index("gh")]
     arrived = exchange(pack(plan, q_rows, k_rows, value_rows, grad_out))
     home = exchange(attend(own_lengths, slot_list, arrived, cap))
@@ -285,9 +312,10 @@
 
 
 def solution(mesh):
-    fine = Mesh(mesh.devices.reshape(-1, SHARERS, mesh.devices.shape[1]), ("gh", "gl", "dp"))
-    grp = ("gh", "gl")
-    rows = P(("gh", "gl", "dp"), None)
+    shape = (-1, SHARERS // CORES, CORES, mesh.devices.shape[1])
+    fine = Mesh(mesh.devices.reshape(shape), ("gh", "zx", "core", "dp"))
+    grp = ("gh", "zx", "core")
+    rows = P(grp + ("dp",), None)
     mapped = jax.shard_map(
         body,
         mesh=fine,
@@ -297,7 +325,7 @@
             rows,
             rows,
             P("dp", None, None),
-            P(("gh", "gl", "dp"), None, None),
+            P(grp + ("dp",), None, None),
             P("dp", grp),
         ),
         out_specs=(rows, rows, rows),

time: 199 us -> 194 us (0.975)
  blocking collectives: 16.2 us -> 79.3 us
  waiting for transfers between devices: 135 us -> 74.6 us
  starting transfers between devices: 20.7 us -> 14.6 us
  local copies, waits for them, and re-layouts: 4.26 us -> 0.83 us
    all_to_all x0 -> x1, blocking collectives: none -> 64.4 us  [exchange(): lax.all_to_all(flat, ('zx', 'dp', 'core'), split_axis=0, concat_axis=0, t...]
    all_to_all x2 -> x1, waiting for transfers between devices: 135 us -> 74.6 us  [exchange(): lax.all_to_all(flat, ('zx', 'dp', 'core'), split_axis=0, concat_axis=0, t...]
    all_to_all x2 -> x1, starting transfers between devices: 20.7 us -> 14.6 us  [exchange(): lax.all_to_all(flat, ('zx', 'dp', 'core'), split_axis=0, concat_axis=0, t...]
    unnamed x9 -> x8, local copies, waits for them, and re-layouts: 4.05 us -> 0.71 us
  transfers between devices with their start and end apart: 2 -> 1, of which waited for: 2 -> 1; matrix products, arithmetic and copies ran while one was open for 0% -> 0% of each run, Pallas kernels for 0% -> 0%
where the time goes in v3:
time: 194 us; the launch traced here: 193 us
  blocking collectives  79.3 us (41%)
  waiting for transfers between devices  74.6 us (38%)
  Pallas kernels  22.5 us (12%)
  starting transfers between devices  14.6 us (8%)
    all_to_all x1, waiting for transfers between devices, exchange(): lax.all_to_all(flat, ('zx', 'dp', 'core'), split_axis=0, concat_axis=0, t...  74.6 us
    all_to_all x1, blocking collectives, exchange(): lax.all_to_all(flat, ('zx', 'dp', 'core'), split_axis=0, concat_axis=0, t...  64.4 us
    pallas_call x1, Pallas kernels, attend(): pl.pallas_call(attend_kernel, in_specs=[pl.BlockSpec(memory_space=pltpu.S...  15.3 us
    all_gather x1, blocking collectives, body(): slot_list = lax.all_gather(recv_slots[0], ('zx', 'core'), axis=0)  14.9 us
    all_to_all x1, starting transfers between devices, exchange(): lax.all_to_all(flat, ('zx', 'dp', 'core'), split_axis=0, concat_axis=0, t...  14.6 us
    pallas_call x1, Pallas kernels, pack(): pl.pallas_call(pack_kernel, in_specs=[VMEM] + [OUTSIDE] * 4, out_specs=OU...  5.1 us
  transfers between devices with their start and end apart: 1, of which 1 were waited for; matrix products, arithmetic and copies ran while one was open for 0% of the time, Pallas kernels for 0%

profile of v3, /device:TPU:1, one launch (start us, length us, event | category | flops | bytes accessed | tf_op | source)
XLA Modules:
  0.0 192.7 jit_solution(9689846666714742972)
XLA Ops:
  0.6 0.0 copy-start
  0.6 0.0 copy-start.1
  0.7 0.7 copy-done.1
  1.3 5.1 %pack.1 = bf16[4,16,2,120,128]{4,3,2,1,0:T(8,128)(2,1)} custom-call(s32[12,1,16]{2,1,0:T(1,128)S(1)} %bitcast.37, bf16[128,4096]{1,0:T(8,128)(2,1)} %q_hbm.1, bf16[128,1024]{1,0:T(8,128)(2,1)} %k_hbm.1, bf16[128,1024]{1,0:T(8,128)(2,1)} %v_hbm.1, bf16[128,4096]{1,0:T(8,128)(2,1)} %g_hbm.1), custom_call_target="tpu_custom_call" | custom-call | tf_op jit(solution)/shard_map/pack/pallas_call | solution.py:242
  6.5 0.0 copy-start.3
  6.5 14.6 %all-to-all-start = ((bf16[128,120,128]{2,1,0:T(8,128)(2,1)}), bf16[128,120,128]{2,1,0:T(8,128)(2,1)}, u32[]{:S(2)}, u32[]{:S(2)}) async-start(bf16[128,120,128]{2,1,0:T(8,128)(2,1)} %bitcast.39), calls=%async_computation | async-start | bytes 7864320 | tf_op jit(solution)/shard_map/all_to_all | solution.py:299
  21.1 0.0 copy-done.3
  21.1 14.9 %all-gather = s32[8,1,128]{2,1,0:T(1,128)S(1)} all-gather(s32[1,1,128]{2,1,0:T(1,128)S(1)} %bitcast.42), channel_id=1, replica_groups=mesh['gh'=4,'zx'=4,'core'=2,'dp'=16] {'zx','core'}, dimensions={0}, use_global_device_ids=true | all-gather | bytes 4608 | tf_op jit(solution)/shard_map/all_gather | solution.py:307
  36.0 0.1 copy.15.rows_of_ref
  36.1 0.0 copy-done
  36.2 74.6 %all-to-all-done = bf16[128,120,128]{2,1,0:T(8,128)(2,1)} async-done(((bf16[128,120,128]{2,1,0:T(8,128)(2,1)}), bf16[128,120,128]{2,1,0:T(8,128)(2,1)}, u32[]{:S(2)}, u32[]{:S(2)}) %all-to-all-start) | async-done | bytes 3932192 | tf_op jit(solution)/shard_map/all_to_all | solution.py:299
  110.7 15.3 %attend.1 = bf16[4,16,2,72,128]{4,3,2,1,0:T(8,128)(2,1)S(1)} custom-call(s32[4]{0:T(128)S(1)} %dynamic-slice_bitcast_fusion.lens_ref, s32[128,8]{1,0:T(8,128)S(1)} %copy.15.rows_of_ref, s32[8,128]{1,0:T(8,128)S(1)} %fusion.1.lanes_of_ref, bf16[4,16,2,120,128]{4,3,2,1,0:T(8,128)(2,1)} %bitcast.9.in_ref), custom_call_target="tpu_custom_call" | custom-call | tf_op jit(solution)/shard_map/attend/pallas_call | solution.py:261
  126.0 0.0 copy-start.2
  126.0 64.4 %all_to_all.10 = bf16[128,72,128]{2,1,0:T(8,128)(2,1)S(1)} all-to-all(bf16[128,72,128]{2,1,0:T(8,128)(2,1)S(1)} %bitcast.36), channel_id=1, replica_groups=mesh['gh'=4,'zx'=4,'core'=2,'dp'=16] {'zx','dp','core'}, dimensions={0} | all-to-all | bytes 4718592 | tf_op jit(solution)/shard_map/all_to_all | solution.py:299
  190.4 0.0 copy-done.2
  190.4 2.1 %settle.1 = (bf16[128,4096]{1,0:T(8,128)(2,1)}, bf16[128,1024]{1,0:T(8,128)(2,1)}, bf16[128,1024]{1,0:T(8,128)(2,1)}) custom-call(s32[12,1,16]{2,1,0:T(1,128)S(1)} %bitcast.38, bf16[4,16,2,72,128]{4,3,2,1,0:T(8,128)(2,1)S(1)} %bitcast.35), custom_call_target="tpu_custom_call" | custom-call | tf_op jit(solution)/shard_map/settle/pallas_call | solution.py:285
  (3 shorter events, 0.0 us)
Async XLA Ops:
  0.6 35.5 %copy-start = (s32[1,4,4]{2,1,0:T(4,128)S(1)}, s32[1,4,4]{2,1,0:T(4,128)}, u32[]{:S(2)}) copy-start(s32[1,4,4]{2,1,0:T(4,128)} %param.11) | copy-start | bytes 196
  0.6 0.7 copy-start.1
  6.5 14.7 %copy-start.3 = (s32[1,128]{1,0:T(1,128)S(1)}, s32[1,128]{1,0:T(1,128)}, u32[]{:S(2)}) copy-start(s32[1,128]{1,0:T(1,128)} %param.13) | copy-start | bytes 1540
  6.5 104.3 %all-to-all-start = ((bf16[128,120,128]{2,1,0:T(8,128)(2,1)}), bf16[128,120,128]{2,1,0:T(8,128)(2,1)}, u32[]{:S(2)}, u32[]{:S(2)}) async-start(bf16[128,120,128]{2,1,0:T(8,128)(2,1)} %bitcast.39), calls=%async_computation | async-start | bytes 7864320 | tf_op jit(solution)/shard_map/all_to_all | solution.py:299
  126.0 64.4 %copy-start.2 = (s32[1,16,12]{1,0,2:T(1,128)S(1)}, s32[1,16,12]{1,0,2:T(1,128)}, u32[]{:S(2)}) copy-start(s32[1,16,12]{1,0,2:T(1,128)} %param.12) | copy-start | bytes 2308

commit v4 on v3

--- a/solution.py
+++ b/solution.py
@@ -58,12 +58,12 @@
     slots = n * cap2
     pairs = ((q_hbm, q_s), (k_hbm, k_s), (v_hbm, v_s), (g_hbm, g_s))
     copies = []
-    for group in range(SHARERS):
+    for part in range(2):
         for i, (source, held) in enumerate(pairs):
-            width = held.shape[1] // SHARERS
-            lanes = pl.ds(group * width, width)
+            width = held.shape[1] // 2
+            lanes = pl.ds(part * width, width)
             copies.append(
-                pltpu.make_async_copy(source.at[:, lanes], held.at[:, lanes], sems.at[group, i])
+                pltpu.make_async_copy(source.at[:, lanes], held.at[:, lanes], sems.at[part, i])
             )
             copies[-1].start()
     want = wanted(plan_ref, rows, False)
@@ -71,8 +71,10 @@
     sends = []
 
     for group in range(SHARERS):
-        for copy in copies[group * 4 : group * 4 + 4]:
-            copy.wait()
+        if group % 4 == 0:
+            part = group // 4
+            for copy in copies[part * 4 : part * 4 + 4]:
+                copy.wait()
 
         def put(pair, block):
             out_s[group // CORES, :, group % CORES, pair * cap2 : (pair + 1) * cap2, :] = (
@@ -86,11 +88,12 @@
             put(pair + 1, both[:, HEAD:])
         lanes = slice(group * HEAD, (group + 1) * HEAD)
         put(PER, dot(pick, jnp.concatenate([k_s[:, lanes], v_s[:, lanes]], axis=0)))
-        block = (group // CORES, slice(None), group % CORES)
-        sends.append(
-            pltpu.make_async_copy(out_s.at[block], out_hbm.at[block], out_sems.at[group])
-        )
-        sends[-1].start()
+        if group % CORES == CORES - 1:
+            block = group // CORES
+            sends.append(
+                pltpu.make_async_copy(out_s.at[block], out_hbm.at[block], out_sems.at[block])
+            )
+            sends[-1].start()
     for send in sends:
         send.wait()
 
@@ -108,7 +111,7 @@
     scale = 1.0 / math.sqrt(HEAD)
     log_scale = scale * math.log2(math.e)
 
-    for group in range(groups):
+    def unpack(group):
         want = rows_of_ref[:, group : group + 1]
         want = jnp.concatenate([want, want + cap], axis=0)
         pick = (want == lax.broadcasted_iota(I32, (2 * rows, slots), 1)).astype(BF)
@@ -129,44 +132,82 @@
         v_s[at, :] = both[rows:].astype(BF)
         kt_s[:, at] = both[:rows].T.astype(BF)
 
+    for group in range(2 * (TILE // rows)):
+        unpack(group)
+
     dk_s[...] = jnp.zeros_like(dk_s)
     dv_s[...] = jnp.zeros_like(dv_s)
     key_at = lax.broadcasted_iota(I32, (column, TILE), 0)
     causal = key_at[:TILE] <= lax.broadcasted_iota(I32, (TILE, TILE), 1)
 
-    for tile in range(column // TILE):
-        old, seen = tile * TILE, (tile + 1) * TILE
-        place = lax.broadcasted_iota(I32, (1, TILE), 1) + old
+    def begin_of(tile):
+        place = lax.broadcasted_iota(I32, (1, TILE), 1) + tile * TILE
         begin = jnp.zeros((1, TILE), I32)
         end = jnp.int32(0)
         for j in range(lens_ref.shape[0]):
             end = end + lens_ref[j]
             begin = jnp.where(end <= place, end, begin)
-
-        def masked(raw):
-            last = jnp.where((key_at[:TILE] >= begin - old) & causal, raw[old:], LOW)
-            if not tile:
-                return last
-            return jnp.concatenate([jnp.where(key_at[:old] >= begin, raw[:old], LOW), last], axis=0)
-
-        queries = [q_s[head, old:seen, :] for head in range(PER)]
-        grads = [g_s[head, old:seen, :] for head in range(PER)]
-        raws = [masked(dot(k_s[:seen, :], query, NT)) for query in queries]
-        d_weights = [dot(v_s[:seen, :], grad, NT) for grad in grads]
+        return begin
+
+    def products(tile, head):
+        old, seen = tile * TILE, (tile + 1) * TILE
+        return (
+            dot(k_s[:seen, :], q_s[head, old:seen, :], NT),
+            dot(v_s[:seen, :], g_s[head, old:seen, :], NT),
+        )
+
+    def softmax(tile, begin, raw, d_weight):
+        old = tile * TILE
+        last = jnp.where((key_at[:TILE] >= begin - old) & causal, raw[old:], LOW)
+        if tile:
+            first = jnp.where(key_at[:old] >= begin, raw[:old], LOW)
+            raw = jnp.concatenate([first, last], axis=0)
+        else:
+            raw = last
+        top = jnp.max(raw, axis=0, keepdims=True)
+        shifted = jnp.exp2((raw - top) * log_scale)
+        total = jnp.sum(shifted, axis=0, keepdims=True)
+        weight = (shifted * (1.0 / total)).astype(BF)
+        weight_f = weight.astype(F32)
+        delta = jnp.sum(weight_f * d_weight, axis=0, keepdims=True)
+        return weight, (weight_f * (d_weight - delta)).astype(BF)
+
+    def spread_out(total_s, tile, left, right):
+        old, seen = tile * TILE, (tile + 1) * TILE
+        total_s[:seen, :] += dot(
+            jnp.concatenate(left, axis=1),
+            jnp.concatenate([right[head, old:seen, :] for head in range(PER)], axis=0),
+        )
+
+    tiles = list(range(column // TILE))
+    made = [products(tiles[0], head) for head in range(PER)]
+    waiting = []
+    for step, tile in enumerate(tiles):
+        old, seen = tile * TILE, (tile + 1) * TILE
+        begin = begin_of(tile)
+        following = []
         weights, dscores = [], []
         for head in range(PER):
-            top = jnp.max(raws[head], axis=0, keepdims=True)
-            shifted = jnp.exp2((raws[head] - top) * log_scale)
-            total = jnp.sum(shifted, axis=0, keepdims=True)
-            weight = (shifted * (1.0 / total)).astype(BF)
-            weight_f = weight.astype(F32)
-            delta = jnp.sum(weight_f * d_weights[head], axis=0, keepdims=True)
-            dscore = (weight_f * (d_weights[head] - delta)).astype(BF)
+            if step + 1 < len(tiles) and False:
+                following.append(products(tiles[step + 1], head))
+            weight, dscore = softmax(tile, begin, *made[head])
+            if step + 2 < len(tiles) and head in (0, 2):
+                unpack((tile + 2) * TILE // rows + head // 2)
+            if step + 1 < len(tiles) and not False:
+                following.append(products(tiles[step + 1], head))
             dqt_s[head, :, old:seen] = (dot(kt_s[:, :seen], dscore) * scale).astype(BF)
             weights.append(weight)
             dscores.append(dscore)
-        dk_s[:seen, :] += dot(jnp.concatenate(dscores, axis=1), jnp.concatenate(queries, axis=0))
-        dv_s[:seen, :] += dot(jnp.concatenate(weights, axis=1), jnp.concatenate(grads, axis=0))
+            if waiting:
+                spread_out(*waiting.pop(0))
+        waiting = [(dk_s, tile, dscores, q_s), (dv_s, tile, weights, g_s)]
+        if not False:
+            for w in waiting:
+                spread_out(*w)
+            waiting = []
+        made = following
+    for w in waiting:
+        spread_out(*w)
 
     dk_b = (dk_s[...] * scale).astype(BF)
     dv_b = dv_s[...].astype(BF)

time: 194 us -> 192 us (0.990)
  Pallas kernels: 22.5 us -> 20.2 us
where the time goes in v4:
time: 192 us; the launch traced here: 190 us
  blocking collectives  79.3 us (41%)
  waiting for transfers between devices  74.6 us (39%)
  Pallas kernels  20.2 us (11%)
  starting transfers between devices  14.6 us (8%)
    all_to_all x1, waiting for transfers between devices, exchange(): lax.all_to_all(flat, ('zx', 'dp', 'core'), split_axis=0, concat_axis=0, t...  74.6 us
    all_to_all x1, blocking collectives, exchange(): lax.all_to_all(flat, ('zx', 'dp', 'core'), split_axis=0, concat_axis=0, t...  64.4 us
    all_gather x1, blocking collectives, body(): slot_list = lax.all_gather(recv_slots[0], ('zx', 'core'), axis=0)  14.9 us
    all_to_all x1, starting transfers between devices, exchange(): lax.all_to_all(flat, ('zx', 'dp', 'core'), split_axis=0, concat_axis=0, t...  14.6 us
    pallas_call x1, Pallas kernels, attend(): pl.pallas_call(attend_kernel, in_specs=[pl.BlockSpec(memory_space=pltpu.S...  13.9 us
    pallas_call x1, Pallas kernels, pack(): pl.pallas_call(pack_kernel, in_specs=[VMEM] + [OUTSIDE] * 4, out_specs=OU...  4.17 us
  transfers between devices with their start and end apart: 1, of which 1 were waited for; matrix products, arithmetic and copies ran while one was open for 0% of the time, Pallas kernels for 0%

profile of v4, /device:TPU:1, one launch (start us, length us, event | category | flops | bytes accessed | tf_op | source)
XLA Modules:
  0.0 190.5 jit_solution(14085187457035564867)
XLA Ops:
  0.6 0.0 copy-start
  0.6 0.0 copy-start.1
  0.7 0.7 copy-done.1
  1.3 4.2 %pack.1 = bf16[4,16,2,120,128]{4,3,2,1,0:T(8,128)(2,1)} custom-call(s32[12,1,16]{2,1,0:T(1,128)S(1)} %bitcast.37, bf16[128,4096]{1,0:T(8,128)(2,1)} %q_hbm.1, bf16[128,1024]{1,0:T(8,128)(2,1)} %k_hbm.1, bf16[128,1024]{1,0:T(8,128)(2,1)} %v_hbm.1, bf16[128,4096]{1,0:T(8,128)(2,1)} %g_hbm.1), custom_call_target="tpu_custom_call" | custom-call | tf_op jit(solution)/shard_map/pack/pallas_call | solution.py:283
  5.5 0.0 copy-start.3
  5.5 14.6 %all-to-all-start = ((bf16[128,120,128]{2,1,0:T(8,128)(2,1)}), bf16[128,120,128]{2,1,0:T(8,128)(2,1)}, u32[]{:S(2)}, u32[]{:S(2)}) async-start(bf16[128,120,128]{2,1,0:T(8,128)(2,1)} %bitcast.39), calls=%async_computation | async-start | bytes 7864320 | tf_op jit(solution)/shard_map/all_to_all | solution.py:340
  20.2 0.0 copy-done.3
  20.2 14.9 %all-gather = s32[8,1,128]{2,1,0:T(1,128)S(1)} all-gather(s32[1,1,128]{2,1,0:T(1,128)S(1)} %bitcast.42), channel_id=1, replica_groups=mesh['gh'=4,'zx'=4,'core'=2,'dp'=16] {'zx','core'}, dimensions={0}, use_global_device_ids=true | all-gather | bytes 4608 | tf_op jit(solution)/shard_map/all_gather | solution.py:348
  35.1 0.1 copy.15.rows_of_ref
  35.2 0.0 copy-done
  35.2 74.6 %all-to-all-done = bf16[128,120,128]{2,1,0:T(8,128)(2,1)} async-done(((bf16[128,120,128]{2,1,0:T(8,128)(2,1)}), bf16[128,120,128]{2,1,0:T(8,128)(2,1)}, u32[]{:S(2)}, u32[]{:S(2)}) %all-to-all-start) | async-done | bytes 3932192 | tf_op jit(solution)/shard_map/all_to_all | solution.py:340
  109.8 13.9 %attend.1 = bf16[4,16,2,72,128]{4,3,2,1,0:T(8,128)(2,1)S(1)} custom-call(s32[4]{0:T(128)S(1)} %dynamic-slice_bitcast_fusion.lens_ref, s32[128,8]{1,0:T(8,128)S(1)} %copy.15.rows_of_ref, s32[8,128]{1,0:T(8,128)S(1)} %fusion.1.lanes_of_ref, bf16[4,16,2,120,128]{4,3,2,1,0:T(8,128)(2,1)} %bitcast.9.in_ref), custom_call_target="tpu_custom_call" | custom-call | tf_op jit(solution)/shard_map/attend/pallas_call | solution.py:302
  123.7 0.0 copy-start.2
  123.8 64.4 %all_to_all.10 = bf16[128,72,128]{2,1,0:T(8,128)(2,1)S(1)} all-to-all(bf16[128,72,128]{2,1,0:T(8,128)(2,1)S(1)} %bitcast.36), channel_id=1, replica_groups=mesh['gh'=4,'zx'=4,'core'=2,'dp'=16] {'zx','dp','core'}, dimensions={0} | all-to-all | bytes 4718592 | tf_op jit(solution)/shard_map/all_to_all | solution.py:340
  188.2 0.0 copy-done.2
  188.2 2.1 %settle.1 = (bf16[128,4096]{1,0:T(8,128)(2,1)}, bf16[128,1024]{1,0:T(8,128)(2,1)}, bf16[128,1024]{1,0:T(8,128)(2,1)}) custom-call(s32[12,1,16]{2,1,0:T(1,128)S(1)} %bitcast.38, bf16[4,16,2,72,128]{4,3,2,1,0:T(8,128)(2,1)S(1)} %bitcast.35), custom_call_target="tpu_custom_call" | custom-call | tf_op jit(solution)/shard_map/settle/pallas_call | solution.py:326
  (3 shorter events, 0.0 us)
Async XLA Ops:
  0.6 34.6 %copy-start = (s32[1,4,4]{2,1,0:T(4,128)S(1)}, s32[1,4,4]{2,1,0:T(4,128)}, u32[]{:S(2)}) copy-start(s32[1,4,4]{2,1,0:T(4,128)} %param.11) | copy-start | bytes 196
  0.6 0.7 copy-start.1
  5.5 14.7 %copy-start.3 = (s32[1,128]{1,0:T(1,128)S(1)}, s32[1,128]{1,0:T(1,128)}, u32[]{:S(2)}) copy-start(s32[1,128]{1,0:T(1,128)} %param.13) | copy-start | bytes 1540
  5.5 104.3 %all-to-all-start = ((bf16[128,120,128]{2,1,0:T(8,128)(2,1)}), bf16[128,120,128]{2,1,0:T(8,128)(2,1)}, u32[]{:S(2)}, u32[]{:S(2)}) async-start(bf16[128,120,128]{2,1,0:T(8,128)(2,1)} %bitcast.39), calls=%async_computation | async-start | bytes 7864320 | tf_op jit(solution)/shard_map/all_to_all | solution.py:340
  123.7 64.4 %copy-start.2 = (s32[1,16,12]{1,0,2:T(1,128)S(1)}, s32[1,16,12]{1,0,2:T(1,128)}, u32[]{:S(2)}) copy-start(s32[1,16,12]{1,0,2:T(1,128)} %param.12) | copy-start | bytes 2308

commit v5 on v4

--- a/solution.py
+++ b/solution.py
@@ -169,8 +169,9 @@
         total = jnp.sum(shifted, axis=0, keepdims=True)
         weight = (shifted * (1.0 / total)).astype(BF)
         weight_f = weight.astype(F32)
-        delta = jnp.sum(weight_f * d_weight, axis=0, keepdims=True)
-        return weight, (weight_f * (d_weight - delta)).astype(BF)
+        product = weight_f * d_weight
+        delta = jnp.sum(product, axis=0, keepdims=True)
+        return weight, (product - weight_f * delta).astype(BF)
 
     def spread_out(total_s, tile, left, right):
         old, seen = tile * TILE, (tile + 1) * TILE

time: 192 us -> 192 us (level)
  no operation moved by 1% of the time
where the time goes in v5:
time: 192 us; the launch traced here: 190 us
  blocking collectives  79.1 us (41%)
  waiting for transfers between devices  74.6 us (39%)
  Pallas kernels  20 us (10%)
  starting transfers between devices  14.6 us (8%)
    all_to_all x1, waiting for transfers between devices, exchange(): lax.all_to_all(flat, ('zx', 'dp', 'core'), split_axis=0, concat_axis=0, t...  74.6 us
    all_to_all x1, blocking collectives, exchange(): lax.all_to_all(flat, ('zx', 'dp', 'core'), split_axis=0, concat_axis=0, t...  64.2 us
    all_gather x1, blocking collectives, body(): slot_list = lax.all_gather(recv_slots[0], ('zx', 'core'), axis=0)  14.9 us
    all_to_all x1, starting transfers between devices, exchange(): lax.all_to_all(flat, ('zx', 'dp', 'core'), split_axis=0, concat_axis=0, t...  14.6 us
    pallas_call x1, Pallas kernels, attend(): pl.pallas_call(attend_kernel, in_specs=[pl.BlockSpec(memory_space=pltpu.S...  13.7 us
    pallas_call x1, Pallas kernels, pack(): pl.pallas_call(pack_kernel, in_specs=[VMEM] + [OUTSIDE] * 4, out_specs=OU...  4.17 us
  transfers between devices with their start and end apart: 1, of which 1 were waited for; matrix products, arithmetic and copies ran while one was open for 0% of the time, Pallas kernels for 0%

profile of v5, /device:TPU:1, one launch (start us, length us, event | category | flops | bytes accessed | tf_op | source)
XLA Modules:
  0.0 190.0 jit_solution(5713756430435816354)
XLA Ops:
  0.6 0.0 copy-start
  0.6 0.0 copy-start.1
  0.7 0.7 copy-done.1
  1.3 4.2 %pack.1 = bf16[4,16,2,120,128]{4,3,2,1,0:T(8,128)(2,1)} custom-call(s32[12,1,16]{2,1,0:T(1,128)S(1)} %bitcast.37, bf16[128,4096]{1,0:T(8,128)(2,1)} %q_hbm.1, bf16[128,1024]{1,0:T(8,128)(2,1)} %k_hbm.1, bf16[128,1024]{1,0:T(8,128)(2,1)} %v_hbm.1, bf16[128,4096]{1,0:T(8,128)(2,1)} %g_hbm.1), custom_call_target="tpu_custom_call" | custom-call | tf_op jit(solution)/shard_map/pack/pallas_call | solution.py:284
  5.5 0.0 copy-start.3
  5.5 14.6 %all-to-all-start = ((bf16[128,120,128]{2,1,0:T(8,128)(2,1)}), bf16[128,120,128]{2,1,0:T(8,128)(2,1)}, u32[]{:S(2)}, u32[]{:S(2)}) async-start(bf16[128,120,128]{2,1,0:T(8,128)(2,1)} %bitcast.39), calls=%async_computation | async-start | bytes 7864320 | tf_op jit(solution)/shard_map/all_to_all | solution.py:341
  20.2 0.0 copy-done.3
  20.2 14.9 %all-gather = s32[8,1,128]{2,1,0:T(1,128)S(1)} all-gather(s32[1,1,128]{2,1,0:T(1,128)S(1)} %bitcast.42), channel_id=1, replica_groups=mesh['gh'=4,'zx'=4,'core'=2,'dp'=16] {'zx','core'}, dimensions={0}, use_global_device_ids=true | all-gather | bytes 4608 | tf_op jit(solution)/shard_map/all_gather | solution.py:349
  35.1 0.1 copy.15.rows_of_ref
  35.2 0.0 copy-done
  35.2 74.6 %all-to-all-done = bf16[128,120,128]{2,1,0:T(8,128)(2,1)} async-done(((bf16[128,120,128]{2,1,0:T(8,128)(2,1)}), bf16[128,120,128]{2,1,0:T(8,128)(2,1)}, u32[]{:S(2)}, u32[]{:S(2)}) %all-to-all-start) | async-done | bytes 3932192 | tf_op jit(solution)/shard_map/all_to_all | solution.py:341
  109.8 13.7 %attend.1 = bf16[4,16,2,72,128]{4,3,2,1,0:T(8,128)(2,1)S(1)} custom-call(s32[4]{0:T(128)S(1)} %dynamic-slice_bitcast_fusion.lens_ref, s32[128,8]{1,0:T(8,128)S(1)} %copy.15.rows_of_ref, s32[8,128]{1,0:T(8,128)S(1)} %fusion.1.lanes_of_ref, bf16[4,16,2,120,128]{4,3,2,1,0:T(8,128)(2,1)} %bitcast.9.in_ref), custom_call_target="tpu_custom_call" | custom-call | tf_op jit(solution)/shard_map/attend/pallas_call | solution.py:303
  123.5 0.0 copy-start.2
  123.5 64.2 %all_to_all.10 = bf16[128,72,128]{2,1,0:T(8,128)(2,1)S(1)} all-to-all(bf16[128,72,128]{2,1,0:T(8,128)(2,1)S(1)} %bitcast.36), channel_id=1, replica_groups=mesh['gh'=4,'zx'=4,'core'=2,'dp'=16] {'zx','dp','core'}, dimensions={0} | all-to-all | bytes 4718592 | tf_op jit(solution)/shard_map/all_to_all | solution.py:341
  187.7 0.0 copy-done.2
  187.7 2.1 %settle.1 = (bf16[128,4096]{1,0:T(8,128)(2,1)}, bf16[128,1024]{1,0:T(8,128)(2,1)}, bf16[128,1024]{1,0:T(8,128)(2,1)}) custom-call(s32[12,1,16]{2,1,0:T(1,128)S(1)} %bitcast.38, bf16[4,16,2,72,128]{4,3,2,1,0:T(8,128)(2,1)S(1)} %bitcast.35), custom_call_target="tpu_custom_call" | custom-call | tf_op jit(solution)/shard_map/settle/pallas_call | solution.py:327
  (3 shorter events, 0.0 us)
Async XLA Ops:
  0.6 34.6 %copy-start = (s32[1,4,4]{2,1,0:T(4,128)S(1)}, s32[1,4,4]{2,1,0:T(4,128)}, u32[]{:S(2)}) copy-start(s32[1,4,4]{2,1,0:T(4,128)} %param.11) | copy-start | bytes 196
  0.6 0.7 copy-start.1
  5.5 14.7 %copy-start.3 = (s32[1,128]{1,0:T(1,128)S(1)}, s32[1,128]{1,0:T(1,128)}, u32[]{:S(2)}) copy-start(s32[1,128]{1,0:T(1,128)} %param.13) | copy-start | bytes 1540
  5.5 104.3 %all-to-all-start = ((bf16[128,120,128]{2,1,0:T(8,128)(2,1)}), bf16[128,120,128]{2,1,0:T(8,128)(2,1)}, u32[]{:S(2)}, u32[]{:S(2)}) async-start(bf16[128,120,128]{2,1,0:T(8,128)(2,1)} %bitcast.39), calls=%async_computation | async-start | bytes 7864320 | tf_op jit(solution)/shard_map/all_to_all | solution.py:341
  123.5 64.2 %copy-start.2 = (s32[1,16,12]{1,0,2:T(1,128)S(1)}, s32[1,16,12]{1,0,2:T(1,128)}, u32[]{:S(2)}) copy-start(s32[1,16,12]{1,0,2:T(1,128)} %param.12) | copy-start | bytes 2308
